TPU v7x, 512 devices: a whole 4x4x16 slice. The times are simulated.
512 devices in a mesh: cell: 128 (over y, x, z_hi, core), gene: 4 (over z_lo).
Axes of the slice: x: 4, y: 4, z: 16 (z_hi: 4, z_lo: 4; z = z_hi * 4 + z_lo), core: 2. Of those that a mesh axis runs over, the one named last changes fastest.
Arguments:
- counts: bfloat16 [262144, 4096], P('cell', 'gene'), may hold values from -14 to 14
- loadings: bfloat16 [4096, 256], P('gene'), may hold values from -0.09375 to 0.09375
- kernel_widths: float32 [8], replicated, may hold values from 0.4 to 1.6
- width_index: int32 [262144], P(('cell', 'gene')), may hold values from 0 to 7
- block_fill: int32 [128], replicated, may hold values from 1 to 2048, 196608 in all
- plan: int32 [2], replicated, may hold values from 1 to 127, as said below
Outputs:
- density: float32 [262144], P(('cell', 'gene'))
- eccentricity: float32 [262144], P(('cell', 'gene'))
Inputs may be any that keep to these rules, and one draw needn't show every extreme that they name: `plan`: the 2 values are distinct and one of them is 127.
All inputs are finite; a program needn't handle non-finite values.
Results may differ from a plain program's by a relative error of at most 0.00031.
Values may be sent and summed in bfloat16 or wider, within the bound.
No kernel may reach another device: no remote copies, remote signals or barrier semaphores. Data moves between devices by JAX's collectives and lax.ppermute only.
A program may use at most 64 MiB of HBM per device.

v0:
```python
import jax
import jax.numpy as jnp
from jax import lax
from jax.sharding import PartitionSpec as P


def from_partner(value, axis, stride):
    mask = 2**stride
    pairs = [(source, source ^ mask) for source in range(lax.axis_size(axis))]
    return lax.ppermute(value, axis, pairs)


def block_terms(queries, coef, keys, fill):
    qf = queries.astype(jnp.float32)
    kf = keys.astype(jnp.float32)
    qnorm = jnp.sum(qf * qf, axis=1)
    knorm = jnp.sum(kf * kf, axis=1)
    inner = jnp.einsum("qc,kc->qk", queries, keys, preferred_element_type=jnp.float32)
    dist = jnp.maximum(qnorm[:, None] + knorm[None, :] - 2.0 * inner, 0.0)
    live = jnp.arange(keys.shape[0], dtype=jnp.int32)[None, :] < fill
    kernel = jnp.where(live, jnp.exp(-dist * coef[:, None]), 0.0)
    return (jnp.sum(kernel, axis=1), jnp.max(jnp.where(live, dist, 0.0), axis=1))


def lookup(table, index):
    slots = jnp.arange(table.shape[0], dtype=jnp.int32)
    return jnp.sum(jnp.where(slots == index, table, 0))


def per_device(counts, loadings, kernel_widths, width_index, block_fill, plan):
    groups = lax.axis_size("gene")
    rows = counts.shape[0]
    share = rows // groups
    gene_pos = lax.axis_index("gene")
    cell_pos = lax.axis_index("cell")
    partial_scores = jnp.dot(counts, loadings, preferred_element_type=jnp.float32)
    whole = lax.psum(partial_scores, "gene").astype(jnp.bfloat16)
    mine = lax.dynamic_slice_in_dim(whole, gene_pos * share, share, 0)
    comps = whole.shape[1]
    picked = width_index[:, None] == jnp.arange(kernel_widths.shape[0], dtype=jnp.int32)[None, :]
    width = jnp.sum(jnp.where(picked, kernel_widths[None, :], 0.0), axis=1)
    coef = 1.0 / (2.0 * comps * width * width)
    own_fill = lookup(block_fill, cell_pos)
    total, top = block_terms(mine, coef, whole, own_fill)
    levels = lax.axis_size("cell").bit_length() - 1
    for step in range(plan.shape[0]):
        stride = plan[step]
        moving = whole
        for bit in range(levels):
            swapped = from_partner(moving, "cell", bit)
            moving = jnp.where(
                jnp.bitwise_and(jnp.right_shift(stride, bit), 1) == 1, swapped, moving
            )
        other_fill = lookup(block_fill, jnp.bitwise_xor(cell_pos, stride))
        more, far = block_terms(mine, coef, moving, other_fill)
        total = total + more
        top = jnp.maximum(top, far)
    positions = gene_pos * share + jnp.arange(share, dtype=jnp.int32)
    qlive = positions < own_fill
    density = jnp.where(qlive, jnp.log(total), 0.0)
    spread = jnp.where(qlive, jnp.sqrt(top / comps), 0.0)
    return (density, spread)


def solution(mesh):
    placed = (P("cell", "gene"), P("gene", None), P(), P(("cell", "gene")), P(), P())
    return jax.shard_map(
        per_device,
        mesh=mesh,
        in_specs=placed,
        out_specs=(P(("cell", "gene")), P(("cell", "gene"))),
        check_vma=False,
    )
```

profile of v0, /device:TPU:1, one launch (start us, length us, event | category | flops | bytes accessed | tf_op | source)
XLA Modules:
  0.0 630.0 jit_solution(10061555222739767846)
XLA Ops:
  0.6 0.0 copy-start
  0.6 0.0 copy-start.2
  0.7 1.0 copy-done
  1.7 4.8 fusion.11
  6.5 74.7 %all-reduce.1 = bf16[2048,256]{1,0:T(8,128)(2,1)S(1)} all-reduce(f32[2048,256]{1,0:T(8,128)} %fusion.11), channel_id=1, replica_groups=mesh['cell'=128,'gene'=4] {'gene'}, use_global_device_ids=true, to_apply=%region_1.2 | all-reduce | flops 524288 | bytes 3145728 | tf_op jit(solution)/shard_map/psum | solution.py:37
  81.1 7.3 %collective-permute-start = (bf16[2048,256]{1,0:T(8,128)(2,1)S(1)}, bf16[2048,256]{1,0:T(8,128)(2,1)}, u32[]{:S(2)}, u32[]{:S(2)}) collective-permute-start(bf16[2048,256]{1,0:T(8,128)(2,1)S(1)} %all-reduce.1), channel_id=1, source_target_pairs={{0,4},{4,0},{8,12},{12,8},{16,20},{20,16},{24,28},{28,24},{32,36},... | collective-permute-start | bytes 3145736 | tf_op jit(solution)/shard_map/ppermute | solution.py:10
  88.4 0.0 copy-done.2
  88.5 0.6 fusion.10
  90.3 0.5 collective-permute-done
  90.8 2.3 broadcast_select_fusion.7
  93.2 9.3 %collective-permute-start.7 = (bf16[2048,256]{1,0:T(8,128)(2,1)}, bf16[2048,256]{1,0:T(8,128)(2,1)}, u32[]{:S(2)}, u32[]{:S(2)}) collective-permute-start(bf16[2048,256]{1,0:T(8,128)(2,1)} %get-tuple-element.12), channel_id=1, source_target_pairs={{0,8},{4,12},{8,0},{12,4},{16,24},{20,28},{24,16},{28,20},{32,40},... | collective-permute-start | bytes 3145736 | tf_op jit(solution)/shard_map/ppermute | solution.py:10
  102.5 1.9 collective-permute-start.1
  105.1 221.7 %collective-permute-done.7 = bf16[2048,256]{1,0:T(8,128)(2,1)} collective-permute-done((bf16[2048,256]{1,0:T(8,128)(2,1)}, bf16[2048,256]{1,0:T(8,128)(2,1)}, u32[]{:S(2)}, u32[]{:S(2)}) %collective-permute-start.7) | collective-permute-done | bytes 1048608 | tf_op jit(solution)/shard_map/ppermute | solution.py:10
  326.8 2.3 broadcast_select_fusion.1
  329.2 11.7 %collective-permute-start.8 = (bf16[2048,256]{1,0:T(8,128)(2,1)}, bf16[2048,256]{1,0:T(8,128)(2,1)}, u32[]{:S(2)}, u32[]{:S(2)}) collective-permute-start(bf16[2048,256]{1,0:T(8,128)(2,1)} %broadcast_select_fusion.1), channel_id=1, source_target_pairs={{0,16},{4,20},{8,24},{12,28},{16,0},{20,4},{24,8},{28,12},{32,48},... | collective-permute-start | bytes 3145736 | tf_op jit(solution)/shard_map/ppermute | solution.py:10
  341.5 30.7 %collective-permute-done.1 = bf16[2048,256]{1,0:T(8,128)(2,1)} collective-permute-done((bf16[2048,256]{1,0:T(8,128)(2,1)S(1)}, bf16[2048,256]{1,0:T(8,128)(2,1)}, u32[]{:S(2)}, u32[]{:S(2)}) %collective-permute-start.1) | collective-permute-done | bytes 1048608 | tf_op jit(solution)/shard_map/ppermute | solution.py:10
  372.2 2.3 broadcast_select_fusion.8
  374.5 11.7 %collective-permute-start.2 = (bf16[2048,256]{1,0:T(8,128)(2,1)}, bf16[2048,256]{1,0:T(8,128)(2,1)}, u32[]{:S(2)}, u32[]{:S(2)}) collective-permute-start(bf16[2048,256]{1,0:T(8,128)(2,1)} %broadcast_select_fusion.8), channel_id=1, source_target_pairs={{0,16},{4,20},{8,24},{12,28},{16,0},{20,4},{24,8},{28,12},{32,48},... | collective-permute-start | bytes 3145736 | tf_op jit(solution)/shard_map/ppermute | solution.py:10
  386.9 0.0 collective-permute-done.8
  386.9 1.3 broadcast_select_fusion.2
  388.2 3.1 collective-permute-start.9
  392.0 78.3 %collective-permute-done.2 = bf16[2048,256]{1,0:T(8,128)(2,1)} collective-permute-done((bf16[2048,256]{1,0:T(8,128)(2,1)}, bf16[2048,256]{1,0:T(8,128)(2,1)}, u32[]{:S(2)}, u32[]{:S(2)}) %collective-permute-start.2) | collective-permute-done | bytes 1048608 | tf_op jit(solution)/shard_map/ppermute | solution.py:10
  470.3 2.3 broadcast_select_fusion.9
  472.6 3.1 collective-permute-start.3
  476.4 0.0 copy-start.3
  476.4 0.0 copy-start.1
  476.4 0.0 copy-start.4
  476.4 0.0 collective-permute-done.9
  476.4 2.3 broadcast_select_fusion.3
  478.8 4.3 collective-permute-start.10
  483.8 15.3 %collective-permute-done.3 = bf16[2048,256]{1,0:T(8,128)(2,1)} collective-permute-done((bf16[2048,256]{1,0:T(8,128)(2,1)}, bf16[2048,256]{1,0:T(8,128)(2,1)}, u32[]{:S(2)}, u32[]{:S(2)}) %collective-permute-start.3) | collective-permute-done | bytes 1048608 | tf_op jit(solution)/shard_map/ppermute | solution.py:10
  499.1 1.3 broadcast_select_fusion.10
  500.4 4.7 collective-permute-start.4
  507.0 16.7 %collective-permute-done.10 = bf16[2048,256]{1,0:T(8,128)(2,1)} collective-permute-done((bf16[2048,256]{1,0:T(8,128)(2,1)}, bf16[2048,256]{1,0:T(8,128)(2,1)}, u32[]{:S(2)}, u32[]{:S(2)}) %collective-permute-start.10) | collective-permute-done | bytes 1048608 | tf_op jit(solution)/shard_map/ppermute | solution.py:10
  523.7 2.3 broadcast_select_fusion.4
  526.1 3.2 collective-permute-start.11
  529.3 0.0 copy-done.3
  529.3 0.8 fusion.5
  531.3 0.0 copy-done.1
  531.3 0.0 copy-done.4
  531.3 0.1 select_reduce_fusion.6
  531.4 14.8 %collective-permute-done.4 = bf16[2048,256]{1,0:T(8,128)(2,1)} collective-permute-done((bf16[2048,256]{1,0:T(8,128)(2,1)S(1)}, bf16[2048,256]{1,0:T(8,128)(2,1)}, u32[]{:S(2)}, u32[]{:S(2)}) %collective-permute-start.4) | collective-permute-done | bytes 1048608 | tf_op jit(solution)/shard_map/ppermute | solution.py:10
  546.2 1.1 broadcast_select_fusion.11
  547.3 3.2 collective-permute-start.5
  550.5 0.3 multiply_reduce_fusion.2
  550.9 0.0 collective-permute-done.11
  550.9 1.3 broadcast_select_fusion.5
  552.2 4.6 collective-permute-start.12
  556.8 1.3 iota_compare_fusion.1
  560.1 0.2 multiply_reduce_fusion.3
  560.2 14.5 %collective-permute-done.5 = bf16[2048,256]{1,0:T(8,128)(2,1)} collective-permute-done((bf16[2048,256]{1,0:T(8,128)(2,1)}, bf16[2048,256]{1,0:T(8,128)(2,1)}, u32[]{:S(2)}, u32[]{:S(2)}) %collective-permute-start.5) | collective-permute-done | bytes 1048608 | tf_op jit(solution)/shard_map/ppermute | solution.py:10
  574.7 1.3 broadcast_select_fusion.12
  576.1 4.8 collective-permute-start.6
  580.9 0.6 iota_compare_fusion.3
  581.5 0.8 subtract_maximum_fusion.2
  582.3 17.4 %collective-permute-done.12 = bf16[2048,256]{1,0:T(8,128)(2,1)} collective-permute-done((bf16[2048,256]{1,0:T(8,128)(2,1)S(1)}, bf16[2048,256]{1,0:T(8,128)(2,1)}, u32[]{:S(2)}, u32[]{:S(2)}) %collective-permute-start.12) | collective-permute-done | bytes 1048608 | tf_op jit(solution)/shard_map/ppermute | solution.py:10
  599.7 1.6 multiply_reduce_fusion
  601.3 2.1 subtract_maximum_fusion
  603.4 18.6 %collective-permute-done.6 = bf16[2048,256]{1,0:T(8,128)(2,1)S(1)} collective-permute-done((bf16[2048,256]{1,0:T(8,128)(2,1)S(1)}, bf16[2048,256]{1,0:T(8,128)(2,1)S(1)}, u32[]{:S(2)}, u32[]{:S(2)}) %collective-permute-start.6) | collective-permute-done | bytes 1048608 | tf_op jit(solution)/shard_map/ppermute | solution.py:10
  622.0 0.4 multiply_reduce_fusion.1
  622.4 5.1 select_reduce_fusion.1
  627.5 1.2 sqrt_select_fusion
  628.8 1.2 log_select_fusion
  (1 shorter events, 0.0 us)
Async XLA Ops:
  0.6 1.0 copy-start
  0.6 87.8 %copy-start.2 = (s32[2]{0:T(128)S(1)}, s32[2]{0:T(128)}, u32[]{:S(2)}) copy-start(s32[2]{0:T(128)} %param.11) | copy-start | bytes 28
  81.1 9.7 %collective-permute-start = (bf16[2048,256]{1,0:T(8,128)(2,1)S(1)}, bf16[2048,256]{1,0:T(8,128)(2,1)}, u32[]{:S(2)}, u32[]{:S(2)}) collective-permute-start(bf16[2048,256]{1,0:T(8,128)(2,1)S(1)} %all-reduce.1), channel_id=1, source_target_pairs={{0,4},{4,0},{8,12},{12,8},{16,20},{20,16},{24,28},{28,24},{32,36},... | collective-permute-start | bytes 3145736 | tf_op jit(solution)/shard_map/ppermute | solution.py:10
  93.2 233.6 %collective-permute-start.7 = (bf16[2048,256]{1,0:T(8,128)(2,1)}, bf16[2048,256]{1,0:T(8,128)(2,1)}, u32[]{:S(2)}, u32[]{:S(2)}) collective-permute-start(bf16[2048,256]{1,0:T(8,128)(2,1)} %get-tuple-element.12), channel_id=1, source_target_pairs={{0,8},{4,12},{8,0},{12,4},{16,24},{20,28},{24,16},{28,20},{32,40},... | collective-permute-start | bytes 3145736 | tf_op jit(solution)/shard_map/ppermute | solution.py:10
  102.5 269.6 %collective-permute-start.1 = (bf16[2048,256]{1,0:T(8,128)(2,1)S(1)}, bf16[2048,256]{1,0:T(8,128)(2,1)}, u32[]{:S(2)}, u32[]{:S(2)}) collective-permute-start(bf16[2048,256]{1,0:T(8,128)(2,1)S(1)} %get-tuple-element.11), channel_id=1, source_target_pairs={{0,8},{4,12},{8,0},{12,4},{16,24},{20,28},{24,16},{28,20},{32,40},... | collective-permute-start | bytes 3145736 | tf_op jit(solution)/shard_map/ppermute | solution.py:10
  329.2 57.7 %collective-permute-start.8 = (bf16[2048,256]{1,0:T(8,128)(2,1)}, bf16[2048,256]{1,0:T(8,128)(2,1)}, u32[]{:S(2)}, u32[]{:S(2)}) collective-permute-start(bf16[2048,256]{1,0:T(8,128)(2,1)} %broadcast_select_fusion.1), channel_id=1, source_target_pairs={{0,16},{4,20},{8,24},{12,28},{16,0},{20,4},{24,8},{28,12},{32,48},... | collective-permute-start | bytes 3145736 | tf_op jit(solution)/shard_map/ppermute | solution.py:10
  374.5 95.8 %collective-permute-start.2 = (bf16[2048,256]{1,0:T(8,128)(2,1)}, bf16[2048,256]{1,0:T(8,128)(2,1)}, u32[]{:S(2)}, u32[]{:S(2)}) collective-permute-start(bf16[2048,256]{1,0:T(8,128)(2,1)} %broadcast_select_fusion.8), channel_id=1, source_target_pairs={{0,16},{4,20},{8,24},{12,28},{16,0},{20,4},{24,8},{28,12},{32,48},... | collective-permute-start | bytes 3145736 | tf_op jit(solution)/shard_map/ppermute | solution.py:10
  388.2 88.2 %collective-permute-start.9 = (bf16[2048,256]{1,0:T(8,128)(2,1)S(1)}, bf16[2048,256]{1,0:T(8,128)(2,1)}, u32[]{:S(2)}, u32[]{:S(2)}) collective-permute-start(bf16[2048,256]{1,0:T(8,128)(2,1)S(1)} %broadcast_select_fusion.2), channel_id=1, source_target_pairs={{0,32},{4,36},{8,40},{12,44},{16,48},{20,52},{24,56},{28,60},{32,0... | collective-permute-start | bytes 3145736 | tf_op jit(solution)/shard_map/ppermute | solution.py:10
  472.6 26.4 %collective-permute-start.3 = (bf16[2048,256]{1,0:T(8,128)(2,1)}, bf16[2048,256]{1,0:T(8,128)(2,1)}, u32[]{:S(2)}, u32[]{:S(2)}) collective-permute-start(bf16[2048,256]{1,0:T(8,128)(2,1)} %broadcast_select_fusion.9), channel_id=1, source_target_pairs={{0,32},{4,36},{8,40},{12,44},{16,48},{20,52},{24,56},{28,60},{32,0... | collective-permute-start | bytes 3145736 | tf_op jit(solution)/shard_map/ppermute | solution.py:10
  476.4 52.9 %copy-start.3 = (s32[128]{0:T(128)S(1)}, s32[128]{0:T(128)}, u32[]{:S(2)}) copy-start(s32[128]{0:T(128)} %param.10) | copy-start | bytes 1540
  476.4 54.9 %copy-start.1 = (s32[512]{0:T(512)S(1)}, s32[512]{0:T(512)}, u32[]{:S(2)}) copy-start(s32[512]{0:T(512)} %param.9) | copy-start | bytes 6148
  476.4 54.9 %copy-start.4 = (f32[8]{0:T(128)S(1)}, f32[8]{0:T(128)}, u32[]{:S(2)}) copy-start(f32[8]{0:T(128)} %param.8) | copy-start | bytes 100
  478.8 45.0 %collective-permute-start.10 = (bf16[2048,256]{1,0:T(8,128)(2,1)}, bf16[2048,256]{1,0:T(8,128)(2,1)}, u32[]{:S(2)}, u32[]{:S(2)}) collective-permute-start(bf16[2048,256]{1,0:T(8,128)(2,1)} %broadcast_select_fusion.3), channel_id=1, source_target_pairs={{0,64},{4,68},{8,72},{12,76},{16,80},{20,84},{24,88},{28,92},{32,9... | collective-permute-start | bytes 3145736 | tf_op jit(solution)/shard_map/ppermute | solution.py:10
  500.4 45.8 %collective-permute-start.4 = (bf16[2048,256]{1,0:T(8,128)(2,1)S(1)}, bf16[2048,256]{1,0:T(8,128)(2,1)}, u32[]{:S(2)}, u32[]{:S(2)}) collective-permute-start(bf16[2048,256]{1,0:T(8,128)(2,1)S(1)} %broadcast_select_fusion.10), channel_id=1, source_target_pairs={{0,64},{4,68},{8,72},{12,76},{16,80},{20,84},{24,88},{28,92},{32,9... | collective-permute-start | bytes 3145736 | tf_op jit(solution)/shard_map/ppermute | solution.py:10
  526.1 24.8 %collective-permute-start.11 = (bf16[2048,256]{1,0:T(8,128)(2,1)}, bf16[2048,256]{1,0:T(8,128)(2,1)}, u32[]{:S(2)}, u32[]{:S(2)}) collective-permute-start(bf16[2048,256]{1,0:T(8,128)(2,1)} %broadcast_select_fusion.4), channel_id=1, source_target_pairs={{0,128},{4,132},{8,136},{12,140},{16,144},{20,148},{24,152},{28,15... | collective-permute-start | bytes 3145736 | tf_op jit(solution)/shard_map/ppermute | solution.py:10
  547.3 27.4 %collective-permute-start.5 = (bf16[2048,256]{1,0:T(8,128)(2,1)}, bf16[2048,256]{1,0:T(8,128)(2,1)}, u32[]{:S(2)}, u32[]{:S(2)}) collective-permute-start(bf16[2048,256]{1,0:T(8,128)(2,1)} %broadcast_select_fusion.11), channel_id=1, source_target_pairs={{0,128},{4,132},{8,136},{12,140},{16,144},{20,148},{24,152},{28,15... | collective-permute-start | bytes 3145736 | tf_op jit(solution)/shard_map/ppermute | solution.py:10
  552.2 47.4 %collective-permute-start.12 = (bf16[2048,256]{1,0:T(8,128)(2,1)S(1)}, bf16[2048,256]{1,0:T(8,128)(2,1)}, u32[]{:S(2)}, u32[]{:S(2)}) collective-permute-start(bf16[2048,256]{1,0:T(8,128)(2,1)S(1)} %broadcast_select_fusion.5), channel_id=1, source_target_pairs={{0,256},{4,260},{8,264},{12,268},{16,272},{20,276},{24,280},{28,28... | collective-permute-start | bytes 3145736 | tf_op jit(solution)/shard_map/ppermute | solution.py:10
  576.1 45.9 %collective-permute-start.6 = (bf16[2048,256]{1,0:T(8,128)(2,1)S(1)}, bf16[2048,256]{1,0:T(8,128)(2,1)S(1)}, u32[]{:S(2)}, u32[]{:S(2)}) collective-permute-start(bf16[2048,256]{1,0:T(8,128)(2,1)S(1)} %broadcast_select_fusion.12), channel_id=1, source_target_pairs={{0,256},{4,260},{8,264},{12,268},{16,272},{20,276},{24,280},{28,28... | collective-permute-start | bytes 3145736 | tf_op jit(solution)/shard_map/ppermute | solution.py:10
where the time goes:
time: 631 us; the launch traced here: 630 us
  waiting for transfers between devices  429 us (68%)
  blocking collectives  74.7 us (12%)
  starting transfers between devices  73 us (12%)
  other arithmetic  28.1 us (4%)
  matrix products  12.7 us (2%)
  between operations  11.3 us (2%)
    ppermute x13, waiting for transfers between devices, from_partner(): return lax.ppermute(value, axis, pairs)  429 us
    psum x1, blocking collectives, per_device(): whole = lax.psum(partial_scores, 'gene').astype(jnp.bfloat16)  74.7 us
    ppermute x13, starting transfers between devices, from_partner(): return lax.ppermute(value, axis, pairs)  73 us
    select_n x11, other arithmetic, per_device(): jnp.where(jnp.bitwise_and(jnp.right_shift(stride, bit), 1) == 1, swapped,...  20.4 us
  transfers between devices with their start and end apart: 13, of which 10 were waited for; matrix products, arithmetic and copies ran while one was open for 4% of the time, Pallas kernels for 0%

commit v1 on v0

v1 whole, which is shorter than its diff:
```python
import jax
import jax.numpy as jnp
from jax import lax
from jax.sharding import PartitionSpec as P


def swapped(value, axis, mask):
    pairs = [(source, source ^ mask) for source in range(lax.axis_size(axis))]
    return lax.ppermute(value, axis, pairs)


def block_terms(queries, coef, keys, first, fill):
    qf = queries.astype(jnp.float32)
    kf = keys.astype(jnp.float32)
    qnorm = jnp.sum(qf * qf, axis=1)
    knorm = jnp.sum(kf * kf, axis=1)
    inner = jnp.einsum("qc,kc->qk", queries, keys, preferred_element_type=jnp.float32)
    dist = jnp.maximum(qnorm[:, None] + knorm[None, :] - 2.0 * inner, 0.0)
    live = first + jnp.arange(keys.shape[0], dtype=jnp.int32)[None, :] < fill
    kernel = jnp.where(live, jnp.exp(-dist * coef[:, None]), 0.0)
    return (jnp.sum(kernel, axis=1), jnp.max(jnp.where(live, dist, 0.0), axis=1))


def lookup(table, index):
    slots = jnp.arange(table.shape[0], dtype=jnp.int32)
    return jnp.sum(jnp.where(slots == index, table, 0))


def per_device(counts, loadings, kernel_widths, width_index, block_fill, plan):
    groups = lax.axis_size("gene")
    blocks = lax.axis_size("cell")
    rows = counts.shape[0]
    share = rows // groups
    gene_pos = lax.axis_index("gene")
    cell_pos = lax.axis_index("cell")
    comps = loadings.shape[1]
    far = blocks - 1
    other = jnp.where(plan[0] == far, plan[1], plan[0])

    picked = width_index[:, None] == jnp.arange(kernel_widths.shape[0], dtype=jnp.int32)[None, :]
    width = jnp.sum(jnp.where(picked, kernel_widths[None, :], 0.0), axis=1)
    coef = 1.0 / (2.0 * comps * width * width)
    coefs = [coef] + [swapped(coef, "gene", d) for d in range(1, groups)]

    def part(position):
        mine = lax.dynamic_slice_in_dim(counts, position * share, share, 0)
        return jnp.dot(mine, loadings, preferred_element_type=jnp.float32)

    arrived = []
    for d in range(groups - 1, 0, -1):
        leaving = part(jnp.bitwise_xor(gene_pos, d)).astype(jnp.float16)
        arrived.append(swapped(leaving, "gene", d))
    summed = part(gene_pos)
    for piece in arrived:
        summed = summed + piece.astype(jnp.float32)
    scores = summed.astype(jnp.bfloat16)

    partner = swapped(scores, "cell", far)
    queries = [scores] + [swapped(scores, "gene", d) for d in range(1, groups)]
    moves = [lambda x, mask=mask: swapped(x, "cell", mask) for mask in range(1, far)]
    second = lax.switch(other - 1, moves, scores)

    own_fill = lookup(block_fill, cell_pos)
    far_fill = lookup(block_fill, jnp.bitwise_xor(cell_pos, far))
    other_fill = lookup(block_fill, jnp.bitwise_xor(cell_pos, other))
    first = gene_pos * share
    sums, tops = [], []
    for q, c in zip(queries, coefs):
        total, top = block_terms(q, c, scores, first, own_fill)
        for keys, fill in ((partner, far_fill), (second, other_fill)):
            more, wide = block_terms(q, c, keys, first, fill)
            total = total + more
            top = jnp.maximum(top, wide)
        sums.append(total)
        tops.append(top)
    total, top = sums[0], tops[0]
    for d in range(1, groups):
        back = swapped(jnp.stack([sums[d], tops[d]]), "gene", d)
        total = total + back[0]
        top = jnp.maximum(top, back[1])

    qlive = first + jnp.arange(share, dtype=jnp.int32) < own_fill
    density = jnp.where(qlive, jnp.log(total), 0.0)
    spread = jnp.where(qlive, jnp.sqrt(top / comps), 0.0)
    return (density, spread)


def solution(mesh):
    placed = (P("cell", "gene"), P("gene", None), P(), P(("cell", "gene")), P(), P())
    return jax.shard_map(
        per_device,
        mesh=mesh,
        in_specs=placed,
        out_specs=(P(("cell", "gene")), P(("cell", "gene"))),
        check_vma=False,
    )
```

time: 631 us -> 156 us (0.25)
  waiting for transfers between devices: 429 us -> 25.1 us
  blocking collectives: 74.7 us -> 0 us
  starting transfers between devices: 73 us -> 100 us
  other arithmetic: 28.1 us -> 6.04 us
  between operations: 11.3 us -> 3.05 us
  matrix products: 12.7 us -> 19.8 us
    ppermute x13 -> x14, waiting for transfers between devices: 429 us -> 25.1 us  [swapped(): return lax.ppermute(value, axis, pairs)]
    psum x1 -> x0, blocking collectives: 74.7 us -> none  [per_device(): whole = lax.psum(partial_scores, 'gene').astype(jnp.bfloat16)]
    ppermute x13 -> x14, starting transfers between devices: 73 us -> 100 us  [swapped(): return lax.ppermute(value, axis, pairs)]
    select_n x12 -> x0, other arithmetic: 21.6 us -> none  [the longest x11 20.4 us: per_device(): jnp.where(jnp.bitwise_and(jnp.right_shift(stride, bit), 1) == 1, swapped,...]
    dot_general x3 -> x12, matrix products: 7.93 us -> 12.9 us  [block_terms(): jnp.einsum('qc,kc->qk', queries, keys, preferred_element_type=jnp.float32)]
  transfers between devices with their start and end apart: 13 -> 14, of which waited for: 10 -> 4; matrix products, arithmetic and copies ran while one was open for 4% -> 16% of each run, Pallas kernels for 0% -> 0%
where the time goes in v1:
time: 156 us; the launch traced here: 155 us
  starting transfers between devices  100 us (64%)
  waiting for transfers between devices  25.1 us (16%)
  matrix products  19.8 us (13%)
  other arithmetic  6.04 us (4%)
  between operations  3.05 us (2%)
    ppermute x14, starting transfers between devices, swapped(): return lax.ppermute(value, axis, pairs)  100 us
    ppermute x14, waiting for transfers between devices, swapped(): return lax.ppermute(value, axis, pairs)  25.1 us
    dot_general x12, matrix products, block_terms(): jnp.einsum('qc,kc->qk', queries, keys, preferred_element_type=jnp.float32)  12.9 us
    dot_general x4, matrix products, part(): return jnp.dot(mine, loadings, preferred_element_type=jnp.float32)  6.94 us
  transfers between devices with their start and end apart: 14, of which 4 were waited for; matrix products, arithmetic and copies ran while one was open for 16% of the time, Pallas kernels for 0%

profile of v1, /device:TPU:1, one launch (start us, length us, event | category | flops | bytes accessed | tf_op | source)
XLA Modules:
  0.0 155.0 jit_solution(8131295911205393846)
XLA Ops:
  0.6 0.0 copy-start
  0.6 0.0 copy-start.1
  0.7 0.0 copy-start.2
  0.7 0.8 select_reduce_fusion.24
  1.5 7.1 %collective-permute-start.137 = (f32[512]{0:T(512)S(1)}, f32[512]{0:T(512)S(1)}, u32[]{:S(2)}, u32[]{:S(2)}) collective-permute-start(f32[512]{0:T(512)S(1)} %fusion.9), channel_id=1, source_target_pairs={{0,3},{1,2},{2,1},{3,0},{4,7},{5,6},{6,5},{7,4},{8,11},{9,10},{10,... | collective-permute-start | bytes 6152 | tf_op jit(solution)/shard_map/ppermute | solution.py:9
  8.6 1.9 %collective-permute-start.134 = (f32[512]{0:T(512)S(1)}, f32[512]{0:T(512)S(1)}, u32[]{:S(2)}, u32[]{:S(2)}) collective-permute-start(f32[512]{0:T(512)S(1)} %fusion.9), channel_id=1, source_target_pairs={{0,2},{1,3},{2,0},{3,1},{4,6},{5,7},{6,4},{7,5},{8,10},{9,11},{10,... | collective-permute-start | bytes 6152 | tf_op jit(solution)/shard_map/ppermute | solution.py:9
  10.5 0.0 copy-done
  10.5 1.7 %convolution_convert_fusion = f16[512,256]{0,1:T(8,128)(2,1)S(1)} fusion(bf16[1024,256]{1,0:T(8,128)(2,1)S(1)} %copy-done, bf16[2048,1024]{1,0:T(8,128)(2,1)} %param.132, s32[]{:T(128)S(6)} %select_n.114), kind=kOutput, calls=%fused_computation.16 | convolution fusion | flops 268566528 | bytes 1835012 | tf_op jit(solution)/shard_map/dot_general | solution.py:47
  12.3 2.2 %collective-permute-start.128 = (f16[512,256]{0,1:T(8,128)(2,1)S(1)}, f16[512,256]{0,1:T(8,128)(2,1)S(1)}, u32[]{:S(2)}, u32[]{:S(2)}) collective-permute-start(f16[512,256]{0,1:T(8,128)(2,1)S(1)} %convolution_convert_fusion), channel_id=1, source_target_pairs={{0,1},{1,0},{2,3},{3,2},{4,5},{5,4},{6,7},{7,6},{8,9},{9,8},{10,11... | collective-permute-start | bytes 786440 | tf_op jit(solution)/shard_map/ppermute | solution.py:9
  14.5 1.7 %convolution_convert_fusion.1 = f16[512,256]{0,1:T(8,128)(2,1)S(1)} fusion(bf16[1024,256]{1,0:T(8,128)(2,1)S(1)} %copy-done, bf16[2048,1024]{1,0:T(8,128)(2,1)} %param.132, s32[]{:T(128)S(6)} %select_n.113), kind=kOutput, calls=%fused_computation.17 | convolution fusion | flops 268566528 | bytes 1835012 | tf_op jit(solution)/shard_map/dot_general | solution.py:47
  16.2 4.0 %collective-permute-start.127 = (f16[512,256]{0,1:T(8,128)(2,1)S(1)}, f16[512,256]{0,1:T(8,128)(2,1)S(1)}, u32[]{:S(2)}, u32[]{:S(2)}) collective-permute-start(f16[512,256]{0,1:T(8,128)(2,1)S(1)} %convolution_convert_fusion.1), channel_id=1, source_target_pairs={{0,2},{1,3},{2,0},{3,1},{4,6},{5,7},{6,4},{7,5},{8,10},{9,11},{10,... | collective-permute-start | bytes 786440 | tf_op jit(solution)/shard_map/ppermute | solution.py:9
  20.2 1.7 %convolution_convert_fusion.2 = f16[512,256]{0,1:T(8,128)(2,1)S(1)} fusion(bf16[1024,256]{1,0:T(8,128)(2,1)S(1)} %copy-done, bf16[2048,1024]{1,0:T(8,128)(2,1)} %param.132, s32[]{:T(128)S(6)} %select_n.112), kind=kOutput, calls=%fused_computation.18 | convolution fusion | flops 268566528 | bytes 1835012 | tf_op jit(solution)/shard_map/dot_general | solution.py:47
  21.9 3.1 %collective-permute-start.126 = (f16[512,256]{0,1:T(8,128)(2,1)S(1)}, f16[512,256]{0,1:T(8,128)(2,1)S(1)}, u32[]{:S(2)}, u32[]{:S(2)}) collective-permute-start(f16[512,256]{0,1:T(8,128)(2,1)S(1)} %convolution_convert_fusion.2), channel_id=1, source_target_pairs={{0,3},{1,2},{2,1},{3,0},{4,7},{5,6},{6,5},{7,4},{8,11},{9,10},{10,... | collective-permute-start | bytes 786440 | tf_op jit(solution)/shard_map/ppermute | solution.py:9
  25.0 0.0 copy-done.1
  25.0 0.6 fusion.25
  27.6 0.0 copy-done.2
  27.6 0.7 fusion.20
  28.2 0.6 fusion.12
  28.8 1.3 fusion.10
  30.1 0.0 collective-permute-done.128
  30.1 2.2 %collective-permute-start.131 = (f32[512]{0:T(512)S(1)}, f32[512]{0:T(512)S(1)}, u32[]{:S(2)}, u32[]{:S(2)}) collective-permute-start(f32[512]{0:T(512)S(1)} %fusion.9), channel_id=1, source_target_pairs={{0,1},{1,0},{2,3},{3,2},{4,5},{5,4},{6,7},{7,6},{8,9},{9,8},{10,11... | collective-permute-start | bytes 6152 | tf_op jit(solution)/shard_map/ppermute | solution.py:9
  32.3 0.0 collective-permute-done.127
  32.3 1.1 collective-permute-done.126
  33.5 1.8 %multiply_reduce_fusion.5 = (f32[512]{0:T(512)S(1)}, bf16[512,256]{0,1:T(8,128)(2,1)S(1)}) fusion(f16[512,256]{0,1:T(8,128)(2,1)S(1)} %collective-permute-done.128, f16[512,256]{0,1:T(8,128)(2,1)S(1)} %collective-permute-done.127, f16[512,256]{0,1:T(8,128)(2,1)S(1)} %collective-permute-done.126, bf16[1024,256]{1,0:T(8,128)(2,1)S(1)} %copy-done, ...), kind=kOutput, calls=%fused_computation.63 | convolution fusion | flops 269745664 | bytes 2623492 | tf_op jit(solution)/shard_map/dot_general | solution.py:47
  35.3 8.6 %collective-permute-start.136 = (bf16[512,256]{0,1:T(8,128)(2,1)S(1)}, bf16[512,256]{0,1:T(8,128)(2,1)S(1)}, u32[]{:S(2)}, u32[]{:S(2)}) collective-permute-start(bf16[512,256]{0,1:T(8,128)(2,1)S(1)} %get-tuple-element.319), channel_id=1, source_target_pairs={{0,3},{1,2},{2,1},{3,0},{4,7},{5,6},{6,5},{7,4},{8,11},{9,10},{10,... | collective-permute-start | bytes 786440 | tf_op jit(solution)/shard_map/ppermute | solution.py:9
  43.8 0.1 copy.140
  44.0 33.9 %conditional.1 = (bf16[512,256]{1,0:T(8,128)(2,1)}) conditional(s32[]{:T(128)} %clamp.3, bf16[512,256]{1,0:T(8,128)(2,1)S(1)} %copy.140, bf16[512,256]{1,0:T(8,128)(2,1)S(1)} %copy.140, bf16[512,256]{1,0:T(8,128)(2,1)S(1)} %copy.140, bf16[512,256]{1,0:T(8,128)(2,1)S(1)} %copy.140, ...), branch_computations={%region_8.9_spmd, %region_9.10_spmd, %region_10.11_spmd, %region_1... | conditional | bytes 1048624 | solution.py:61
  44.0 23.6 %collective-permute-start.47 = (bf16[512,256]{1,0:T(8,128)(2,1)S(1)}, bf16[512,256]{1,0:T(8,128)(2,1)}, u32[]{:S(2)}, u32[]{:S(2)}) collective-permute-start(bf16[512,256]{1,0:T(8,128)(2,1)S(1)} %param.47), channel_id=1, source_target_pairs={{0,192},{4,196},{8,200},{12,204},{16,208},{20,212},{24,216},{28,22... | collective-permute-start | bytes 786440 | tf_op jit(solution)/shard_map/cond/branch_47_fun/ppermute | solution.py:9
  67.6 10.3 %collective-permute-done.47 = bf16[512,256]{1,0:T(8,128)(2,1)} collective-permute-done((bf16[512,256]{1,0:T(8,128)(2,1)S(1)}, bf16[512,256]{1,0:T(8,128)(2,1)}, u32[]{:S(2)}, u32[]{:S(2)}) %collective-permute-start.47) | collective-permute-done | bytes 262176 | tf_op jit(solution)/shard_map/cond/branch_47_fun/ppermute | solution.py:9
  77.8 17.3 %collective-permute-start.129 = (bf16[512,256]{0,1:T(8,128)(2,1)S(1)}, bf16[512,256]{0,1:T(8,128)(2,1)S(1)}, u32[]{:S(2)}, u32[]{:S(2)}) collective-permute-start(bf16[512,256]{0,1:T(8,128)(2,1)S(1)} %get-tuple-element.319), channel_id=1, source_target_pairs={{0,508},{4,504},{8,500},{12,496},{16,492},{20,488},{24,484},{28,48... | collective-permute-start | bytes 786440 | tf_op jit(solution)/shard_map/ppermute | solution.py:9
  95.1 1.1 multiply_reduce_fusion.3
  96.2 0.3 fusion.2
  96.6 1.3 fusion.3
  97.8 0.0 collective-permute-done.136
  97.8 4.6 %collective-permute-start.133 = (bf16[512,256]{0,1:T(8,128)(2,1)S(1)}, bf16[512,256]{0,1:T(8,128)(2,1)S(1)}, u32[]{:S(2)}, u32[]{:S(2)}) collective-permute-start(bf16[512,256]{0,1:T(8,128)(2,1)S(1)} %get-tuple-element.319), channel_id=1, source_target_pairs={{0,2},{1,3},{2,0},{3,1},{4,6},{5,7},{6,4},{7,5},{8,10},{9,11},{10,... | collective-permute-start | bytes 786440 | tf_op jit(solution)/shard_map/ppermute | solution.py:9
  102.4 0.1 multiply_reduce_fusion
  102.5 1.2 convolution_multiply_fusion
  103.8 0.3 convolution_multiply_fusion.5
  104.1 12.5 %collective-permute-done.129 = bf16[512,256]{0,1:T(8,128)(2,1)S(1)} collective-permute-done((bf16[512,256]{0,1:T(8,128)(2,1)S(1)}, bf16[512,256]{0,1:T(8,128)(2,1)S(1)}, u32[]{:S(2)}, u32[]{:S(2)}) %collective-permute-start.129) | collective-permute-done | bytes 262176 | tf_op jit(solution)/shard_map/ppermute | solution.py:9
  116.6 12.1 %collective-permute-start.130 = (bf16[512,256]{0,1:T(8,128)(2,1)S(1)}, bf16[512,256]{0,1:T(8,128)(2,1)S(1)}, u32[]{:S(2)}, u32[]{:S(2)}) collective-permute-start(bf16[512,256]{0,1:T(8,128)(2,1)S(1)} %get-tuple-element.319), channel_id=1, source_target_pairs={{0,1},{1,0},{2,3},{3,2},{4,5},{5,4},{6,7},{7,6},{8,9},{9,8},{10,11... | collective-permute-start | bytes 786440 | tf_op jit(solution)/shard_map/ppermute | solution.py:9
  128.8 0.1 multiply_reduce_fusion.4
  128.8 0.0 collective-permute-done.137
  128.8 2.0 %select_reduce_fusion.7 = (f32[512]{0:T(512)S(1)}, f32[512]{0:T(512)S(1)}, f32[512]{0:T(512)S(1)}, f32[512]{0:T(512)S(1)}, f32[512]{0:T(512)S(1)}, /*index=5*/f32[512]{0:T(512)S(1)}, f32[512]{0:T(512)S(1)}, f32[512]{0:T(512)S(1)}) fusion(f32[512]{0:T(512)S(1)} %collective-permute-done.137, f32[512]{0:T(512)S(1)} %multiply_reduce_fusion, ...), kind=kOutput, calls=%fused_computation.27 | convolution fusion | flops 143126528 | bytes 3700224 | tf_op jit(solution)/shard_map/qc,kc->qk/dot_general | solution.py:17
  130.9 7.5 %collective-permute-start.138 = (f32[2,512]{1,0:T(2,128)S(1)}, f32[2,512]{1,0:T(2,128)S(1)}, u32[]{:S(2)}, u32[]{:S(2)}) collective-permute-start(f32[2,512]{1,0:T(2,128)S(1)} %pad_maximum_fusion.2), channel_id=1, source_target_pairs={{0,3},{1,2},{2,1},{3,0},{4,7},{5,6},{6,5},{7,4},{8,11},{9,10},{10,... | collective-permute-start | bytes 12296 | tf_op jit(solution)/shard_map/ppermute | solution.py:9
  138.4 0.0 collective-permute-done.133
  138.4 0.1 multiply_reduce_fusion.1
  138.5 1.2 convolution_multiply_fusion.1
  139.7 0.3 convolution_multiply_fusion.10
  140.1 0.0 collective-permute-done.130
  140.1 0.3 convolution_multiply_fusion.9
  140.4 1.2 convolution_multiply_fusion.2
  141.7 0.3 convolution_multiply_fusion.8
  142.1 0.3 convolution_multiply_fusion.7
  142.4 0.1 multiply_reduce_fusion.2
  142.5 0.0 collective-permute-done.134
  142.5 0.0 collective-permute-done.131
  142.5 3.9 %select_reduce_fusion.13 = (f32[512]{0:T(512)S(1)}, f32[512]{0:T(512)S(1)}, f32[512]{0:T(512)S(1)}, f32[512]{0:T(512)S(1)}, f32[512]{0:T(512)S(1)}, /*index=5*/f...) fusion(f32[512]{0:T(512)S(1)} %collective-permute-done.134, ...), kind=kOutput, calls=%fused_computation.36 | convolution fusion | flops 152559616 | bytes 7915008 | tf_op jit(solution)/shard_map/qc,kc->qk/dot_general | solution.py:17
  146.4 3.0 %collective-permute-start.135 = (f32[2,512]{1,0:T(2,128)S(1)}, f32[2,512]{1,0:T(2,128)S(1)}, u32[]{:S(2)}, u32[]{:S(2)}) collective-permute-start(f32[2,512]{1,0:T(2,128)S(1)} %pad_maximum_fusion.1), channel_id=1, source_target_pairs={{0,2},{1,3},{2,0},{3,1},{4,6},{5,7},{6,4},{7,5},{8,10},{9,11},{10,... | collective-permute-start | bytes 12296 | tf_op jit(solution)/shard_map/ppermute | solution.py:9
  149.5 3.0 %collective-permute-start.132 = (f32[2,512]{1,0:T(2,128)S(1)}, f32[2,512]{1,0:T(2,128)S(1)}, u32[]{:S(2)}, u32[]{:S(2)}) collective-permute-start(f32[2,512]{1,0:T(2,128)S(1)} %pad_maximum_fusion), channel_id=1, source_target_pairs={{0,1},{1,0},{2,3},{3,2},{4,5},{5,4},{6,7},{7,6},{8,9},{9,8},{10,11... | collective-permute-start | bytes 12296 | tf_op jit(solution)/shard_map/ppermute | solution.py:9
  152.5 0.0 collective-permute-done.138
  152.5 0.0 collective-permute-done.135
  152.6 1.3 collective-permute-done.132
  153.8 1.2 sqrt_select_fusion
  (13 shorter events, 0.1 us)
Async XLA Ops:
  0.6 9.9 %copy-start = (bf16[1024,256]{1,0:T(8,128)(2,1)S(1)}, bf16[1024,256]{1,0:T(8,128)(2,1)}, u32[]{:S(2)}) copy-start(bf16[1024,256]{1,0:T(8,128)(2,1)} %param.133) | copy-start | bytes 1572868
  0.6 24.4 %copy-start.1 = (s32[2]{0:T(128)S(1)}, s32[2]{0:T(128)}, u32[]{:S(2)}) copy-start(s32[2]{0:T(128)} %param.137) | copy-start | bytes 28
  0.7 26.9 %copy-start.2 = (s32[128]{0:T(128)S(1)}, s32[128]{0:T(128)}, u32[]{:S(2)}) copy-start(s32[128]{0:T(128)} %param.136) | copy-start | bytes 1540
  1.5 127.3 %collective-permute-start.137 = (f32[512]{0:T(512)S(1)}, f32[512]{0:T(512)S(1)}, u32[]{:S(2)}, u32[]{:S(2)}) collective-permute-start(f32[512]{0:T(512)S(1)} %fusion.9), channel_id=1, source_target_pairs={{0,3},{1,2},{2,1},{3,0},{4,7},{5,6},{6,5},{7,4},{8,11},{9,10},{10,... | collective-permute-start | bytes 6152 | tf_op jit(solution)/shard_map/ppermute | solution.py:9
  8.6 133.9 %collective-permute-start.134 = (f32[512]{0:T(512)S(1)}, f32[512]{0:T(512)S(1)}, u32[]{:S(2)}, u32[]{:S(2)}) collective-permute-start(f32[512]{0:T(512)S(1)} %fusion.9), channel_id=1, source_target_pairs={{0,2},{1,3},{2,0},{3,1},{4,6},{5,7},{6,4},{7,5},{8,10},{9,11},{10,... | collective-permute-start | bytes 6152 | tf_op jit(solution)/shard_map/ppermute | solution.py:9
  12.3 17.9 %collective-permute-start.128 = (f16[512,256]{0,1:T(8,128)(2,1)S(1)}, f16[512,256]{0,1:T(8,128)(2,1)S(1)}, u32[]{:S(2)}, u32[]{:S(2)}) collective-permute-start(f16[512,256]{0,1:T(8,128)(2,1)S(1)} %convolution_convert_fusion), channel_id=1, source_target_pairs={{0,1},{1,0},{2,3},{3,2},{4,5},{5,4},{6,7},{7,6},{8,9},{9,8},{10,11... | collective-permute-start | bytes 786440 | tf_op jit(solution)/shard_map/ppermute | solution.py:9
  16.2 16.2 %collective-permute-start.127 = (f16[512,256]{0,1:T(8,128)(2,1)S(1)}, f16[512,256]{0,1:T(8,128)(2,1)S(1)}, u32[]{:S(2)}, u32[]{:S(2)}) collective-permute-start(f16[512,256]{0,1:T(8,128)(2,1)S(1)} %convolution_convert_fusion.1), channel_id=1, source_target_pairs={{0,2},{1,3},{2,0},{3,1},{4,6},{5,7},{6,4},{7,5},{8,10},{9,11},{10,... | collective-permute-start | bytes 786440 | tf_op jit(solution)/shard_map/ppermute | solution.py:9
  21.9 11.5 %collective-permute-start.126 = (f16[512,256]{0,1:T(8,128)(2,1)S(1)}, f16[512,256]{0,1:T(8,128)(2,1)S(1)}, u32[]{:S(2)}, u32[]{:S(2)}) collective-permute-start(f16[512,256]{0,1:T(8,128)(2,1)S(1)} %convolution_convert_fusion.2), channel_id=1, source_target_pairs={{0,3},{1,2},{2,1},{3,0},{4,7},{5,6},{6,5},{7,4},{8,11},{9,10},{10,... | collective-permute-start | bytes 786440 | tf_op jit(solution)/shard_map/ppermute | solution.py:9
  30.1 112.4 %collective-permute-start.131 = (f32[512]{0:T(512)S(1)}, f32[512]{0:T(512)S(1)}, u32[]{:S(2)}, u32[]{:S(2)}) collective-permute-start(f32[512]{0:T(512)S(1)} %fusion.9), channel_id=1, source_target_pairs={{0,1},{1,0},{2,3},{3,2},{4,5},{5,4},{6,7},{7,6},{8,9},{9,8},{10,11... | collective-permute-start | bytes 6152 | tf_op jit(solution)/shard_map/ppermute | solution.py:9
  35.3 62.6 %collective-permute-start.136 = (bf16[512,256]{0,1:T(8,128)(2,1)S(1)}, bf16[512,256]{0,1:T(8,128)(2,1)S(1)}, u32[]{:S(2)}, u32[]{:S(2)}) collective-permute-start(bf16[512,256]{0,1:T(8,128)(2,1)S(1)} %get-tuple-element.319), channel_id=1, source_target_pairs={{0,3},{1,2},{2,1},{3,0},{4,7},{5,6},{6,5},{7,4},{8,11},{9,10},{10,... | collective-permute-start | bytes 786440 | tf_op jit(solution)/shard_map/ppermute | solution.py:9
  44.0 33.8 %collective-permute-start.47 = (bf16[512,256]{1,0:T(8,128)(2,1)S(1)}, bf16[512,256]{1,0:T(8,128)(2,1)}, u32[]{:S(2)}, u32[]{:S(2)}) collective-permute-start(bf16[512,256]{1,0:T(8,128)(2,1)S(1)} %param.47), channel_id=1, source_target_pairs={{0,192},{4,196},{8,200},{12,204},{16,208},{20,212},{24,216},{28,22... | collective-permute-start | bytes 786440 | tf_op jit(solution)/shard_map/cond/branch_47_fun/ppermute | solution.py:9
  77.8 38.8 %collective-permute-start.129 = (bf16[512,256]{0,1:T(8,128)(2,1)S(1)}, bf16[512,256]{0,1:T(8,128)(2,1)S(1)}, u32[]{:S(2)}, u32[]{:S(2)}) collective-permute-start(bf16[512,256]{0,1:T(8,128)(2,1)S(1)} %get-tuple-element.319), channel_id=1, source_target_pairs={{0,508},{4,504},{8,500},{12,496},{16,492},{20,488},{24,484},{28,48... | collective-permute-start | bytes 786440 | tf_op jit(solution)/shard_map/ppermute | solution.py:9
  97.8 40.6 %collective-permute-start.133 = (bf16[512,256]{0,1:T(8,128)(2,1)S(1)}, bf16[512,256]{0,1:T(8,128)(2,1)S(1)}, u32[]{:S(2)}, u32[]{:S(2)}) collective-permute-start(bf16[512,256]{0,1:T(8,128)(2,1)S(1)} %get-tuple-element.319), channel_id=1, source_target_pairs={{0,2},{1,3},{2,0},{3,1},{4,6},{5,7},{6,4},{7,5},{8,10},{9,11},{10,... | collective-permute-start | bytes 786440 | tf_op jit(solution)/shard_map/ppermute | solution.py:9
  116.6 23.5 %collective-permute-start.130 = (bf16[512,256]{0,1:T(8,128)(2,1)S(1)}, bf16[512,256]{0,1:T(8,128)(2,1)S(1)}, u32[]{:S(2)}, u32[]{:S(2)}) collective-permute-start(bf16[512,256]{0,1:T(8,128)(2,1)S(1)} %get-tuple-element.319), channel_id=1, source_target_pairs={{0,1},{1,0},{2,3},{3,2},{4,5},{5,4},{6,7},{7,6},{8,9},{9,8},{10,11... | collective-permute-start | bytes 786440 | tf_op jit(solution)/shard_map/ppermute | solution.py:9
  130.9 21.6 %collective-permute-start.138 = (f32[2,512]{1,0:T(2,128)S(1)}, f32[2,512]{1,0:T(2,128)S(1)}, u32[]{:S(2)}, u32[]{:S(2)}) collective-permute-start(f32[2,512]{1,0:T(2,128)S(1)} %pad_maximum_fusion.2), channel_id=1, source_target_pairs={{0,3},{1,2},{2,1},{3,0},{4,7},{5,6},{6,5},{7,4},{8,11},{9,10},{10,... | collective-permute-start | bytes 12296 | tf_op jit(solution)/shard_map/ppermute | solution.py:9
  146.4 6.1 %collective-permute-start.135 = (f32[2,512]{1,0:T(2,128)S(1)}, f32[2,512]{1,0:T(2,128)S(1)}, u32[]{:S(2)}, u32[]{:S(2)}) collective-permute-start(f32[2,512]{1,0:T(2,128)S(1)} %pad_maximum_fusion.1), channel_id=1, source_target_pairs={{0,2},{1,3},{2,0},{3,1},{4,6},{5,7},{6,4},{7,5},{8,10},{9,11},{10,... | collective-permute-start | bytes 12296 | tf_op jit(solution)/shard_map/ppermute | solution.py:9
  149.5 4.4 %collective-permute-start.132 = (f32[2,512]{1,0:T(2,128)S(1)}, f32[2,512]{1,0:T(2,128)S(1)}, u32[]{:S(2)}, u32[]{:S(2)}) collective-permute-start(f32[2,512]{1,0:T(2,128)S(1)} %pad_maximum_fusion), channel_id=1, source_target_pairs={{0,1},{1,0},{2,3},{3,2},{4,5},{5,4},{6,7},{7,6},{8,9},{9,8},{10,11... | collective-permute-start | bytes 12296 | tf_op jit(solution)/shard_map/ppermute | solution.py:9

commit v2 on v0

v2 whole, which is shorter than its diff:
```python
import functools

import jax
import jax.numpy as jnp
from jax import lax
from jax.experimental import pallas as pl
from jax.experimental.pallas import tpu as pltpu
from jax.sharding import PartitionSpec as P

EXTRA = 16
BIG = 1e30
LOG2E = 1.4426950408889634


def swapped(value, axis, mask):
    pairs = [(source, source ^ mask) for source in range(lax.axis_size(axis))]
    return lax.ppermute(value, axis, pairs)


def chosen(value, axis, index, unit, count):
    moves = [lambda x: x]
    for step in range(1, count):
        moves.append(lambda x, mask=step * unit: swapped(x, axis, mask))
    return lax.switch(index, moves, value)


def squares(x):
    xf = x.astype(jnp.float32)
    square = xf * xf
    high = square.astype(jnp.bfloat16)
    low = (square - high.astype(jnp.float32)).astype(jnp.bfloat16)
    return high, low


def across(a, b):
    return lax.dot_general(a, b, (((1,), (1,)), ((), ())), preferred_element_type=jnp.float32)


def terms_kernel(share, comps, where_ref, fill_ref, widths_ref, query_ref, own_ref, far_ref, other_ref, out_ref, near_ref, wide_ref, twice_ref):
    first = where_ref[0]
    keys = (own_ref, far_ref, other_ref)

    @pl.when(pl.program_id(0) == 0)
    def _():
        ones = jnp.ones((128, comps), jnp.bfloat16)
        slot = first + lax.broadcasted_iota(jnp.int32, (share, 128), 0)
        for n, key_ref in enumerate(keys):
            block = key_ref[...]
            high, low = squares(block)
            norm = across(high, ones) + across(low, ones)
            live = slot < fill_ref[where_ref[1 + n]]
            near_ref[n] = jnp.where(live, norm, BIG)
            wide_ref[n] = jnp.where(live, norm, -BIG)
            twice_ref[n] = block * jnp.bfloat16(-2)

    query = query_ref[0, :share, :]
    high, low = squares(query)
    ones = jnp.ones((8, comps), jnp.bfloat16)
    norm = (across(ones, high) + across(ones, low))[:1]
    index = query_ref[0, share:, :].astype(jnp.float32)
    index = jnp.concatenate([index[row : row + 1] for row in range(share // comps)], axis=1)
    width = jnp.zeros((1, share), jnp.float32)
    for n in range(widths_ref.shape[0]):
        width = jnp.where(index == float(n), widths_ref[n], width)
    coef = -LOG2E / (2.0 * comps * width * width)

    total = jnp.zeros((8, share), jnp.float32)
    top = jnp.full((8, share), -BIG, jnp.float32)
    for n in range(len(keys)):
        inner = across(twice_ref[n], query)
        near = jnp.concatenate([near_ref[n]] * (share // 128), axis=1)
        wide = jnp.concatenate([wide_ref[n]] * (share // 128), axis=1)
        dist = jnp.maximum(inner + near + norm, 0.0)
        kernel = jnp.exp2(dist * coef)
        total = total + jnp.sum(kernel.reshape(share // 8, 8, share), axis=0)
        top = jnp.maximum(top, jnp.max((inner + wide).reshape(share // 8, 8, share), axis=0))
    out_ref[0, 0:1, :] = jnp.sum(total, axis=0, keepdims=True)
    out_ref[0, 1:2, :] = jnp.maximum(jnp.max(top, axis=0, keepdims=True) + norm, 0.0)


def block_terms(where, fill, widths, queries, own, far, other):
    groups, padded, comps = queries.shape
    share = own.shape[0]
    whole = pl.BlockSpec((share, comps), lambda j: (0, 0))
    smem = pl.BlockSpec(memory_space=pltpu.SMEM)
    return pl.pallas_call(
        functools.partial(terms_kernel, share, comps),
        grid=(groups,),
        out_shape=jax.ShapeDtypeStruct((groups, 2, share), jnp.float32),
        in_specs=[smem, smem, smem, pl.BlockSpec((1, padded, comps), lambda j: (j, 0, 0)), whole, whole, whole],
        out_specs=pl.BlockSpec((1, 2, share), lambda j: (j, 0, 0)),
        scratch_shapes=[
            pltpu.VMEM((3, share, 128), jnp.float32),
            pltpu.VMEM((3, share, 128), jnp.float32),
            pltpu.VMEM((3, share, comps), jnp.bfloat16),
        ],
        compiler_params=pltpu.CompilerParams(vmem_limit_bytes=32 * 1024 * 1024),
    )(where, fill, widths, queries, own, far, other)


def per_device(counts, loadings, kernel_widths, width_index, block_fill, plan):
    groups = lax.axis_size("gene")
    blocks = lax.axis_size("cell")
    rows = counts.shape[0]
    share = rows // groups
    gene_pos = lax.axis_index("gene")
    cell_pos = lax.axis_index("cell")
    comps = loadings.shape[1]
    far = blocks - 1
    other = jnp.where(plan[0] == far, plan[1], plan[0])
    first = gene_pos * share
    where = jnp.stack([first, cell_pos, jnp.bitwise_xor(cell_pos, far), jnp.bitwise_xor(cell_pos, other)])

    def part(shard, chunk):
        begin = jnp.bitwise_xor(gene_pos, shard) * share + chunk * half
        mine = lax.dynamic_slice_in_dim(counts, begin, half, 0)
        return jnp.dot(mine, loadings, preferred_element_type=jnp.float32)

    def narrow(x):
        return lax.reduce_precision(x, 8, 10).astype(jnp.float16)

    chunks = 2
    half = share // chunks
    near = [swapped(jnp.concatenate([narrow(part(1, c)), narrow(part(3, c))]), "gene", 1) for c in range(chunks)]
    kept = [(part(0, c), part(2, c)) for c in range(chunks)]
    wide = [swapped(narrow(kept[c][1] + near[c][half:].astype(jnp.float32)), "gene", 2) for c in range(chunks)]
    summed = jnp.concatenate([kept[c][0] + near[c][:half].astype(jnp.float32) + wide[c].astype(jnp.float32) for c in range(chunks)])
    scores = summed.astype(jnp.bfloat16)

    index = jnp.pad(width_index.astype(jnp.bfloat16).reshape(-1, comps), ((0, EXTRA - share // comps), (0, 0)))
    partner = swapped(scores, "cell", far)
    message = jnp.concatenate([scores, index], axis=0)
    queries = lax.all_to_all(jnp.broadcast_to(message[None], (groups,) + message.shape), "gene", 0, 0)
    low = 8
    second = chosen(scores, "cell", other // low, low, blocks // low)
    second = chosen(second, "cell", other % low, 1, low)

    terms = block_terms(where, block_fill, kernel_widths, queries, scores, partner, second)
    both = lax.all_to_all(terms, "gene", 0, 0)
    total = jnp.sum(both[:, 0], axis=0)
    top = jnp.max(both[:, 1], axis=0)
    qlive = first + jnp.arange(share, dtype=jnp.int32) < block_fill[cell_pos]
    density = jnp.where(qlive, jnp.log(total), 0.0)
    spread = jnp.where(qlive, jnp.sqrt(top / comps), 0.0)
    return (density, spread)


def solution(mesh):
    placed = (P("cell", "gene"), P("gene", None), P(), P(("cell", "gene")), P(), P())
    return jax.shard_map(
        per_device,
        mesh=mesh,
        in_specs=placed,
        out_specs=(P(("cell", "gene")), P(("cell", "gene"))),
        check_vma=False,
    )
```

time: 631 us -> 106 us (0.17)
  waiting for transfers between devices: 429 us -> 27.3 us
  blocking collectives: 74.7 us -> 0 us
  other arithmetic: 28.1 us -> 1.66 us
  starting transfers between devices: 73 us -> 51 us
  between operations: 11.3 us -> 2.87 us
  Pallas kernels: 0 us -> 7.09 us
    ppermute x13 -> x7, waiting for transfers between devices: 429 us -> 23.3 us  [swapped(): return lax.ppermute(value, axis, pairs)]
    psum x1 -> x0, blocking collectives: 74.7 us -> none  [per_device(): whole = lax.psum(partial_scores, 'gene').astype(jnp.bfloat16)]
    ppermute x13 -> x7, starting transfers between devices: 73 us -> 33.6 us  [swapped(): return lax.ppermute(value, axis, pairs)]
    select_n x12 -> x0, other arithmetic: 21.6 us -> none  [the longest x11 20.4 us: per_device(): jnp.where(jnp.bitwise_and(jnp.right_shift(stride, bit), 1) == 1, swapped,...]
    all_to_all x0 -> x2, starting transfers between devices: none -> 17.5 us  [the longest x1 13.9 us: per_device(): both = lax.all_to_all(terms, 'gene', 0, 0)]
    pallas_call x0 -> x1, Pallas kernels: none -> 7.09 us  [block_terms(): pl.pallas_call(functools.partial(terms_kernel, share, comps), grid=(group...]
    dot_general x4 -> x8, matrix products: 12.7 us -> 10.9 us  [part(): return jnp.dot(mine, loadings, preferred_element_type=jnp.float32)]
  transfers between devices with their start and end apart: 13 -> 9, of which waited for: 10 -> 5; matrix products, arithmetic and copies ran while one was open for 4% -> 10% of each run, Pallas kernels for 0% -> 0%
where the time goes in v2:
time: 106 us; the launch traced here: 105 us
  starting transfers between devices  51 us (48%)
  waiting for transfers between devices  27.3 us (26%)
  matrix products  10.9 us (10%)
  Pallas kernels  7.09 us (7%)
  local copies, waits for them, and re-layouts  4.04 us (4%)
  between operations  2.87 us (3%)
  other arithmetic  1.66 us (2%)
    ppermute x7, starting transfers between devices, swapped(): return lax.ppermute(value, axis, pairs)  33.6 us
    ppermute x7, waiting for transfers between devices, swapped(): return lax.ppermute(value, axis, pairs)  23.3 us
    all_to_all x1, starting transfers between devices, per_device(): both = lax.all_to_all(terms, 'gene', 0, 0)  13.9 us
    dot_general x8, matrix products, part(): return jnp.dot(mine, loadings, preferred_element_type=jnp.float32)  10.9 us
    pallas_call x1, Pallas kernels, block_terms(): pl.pallas_call(functools.partial(terms_kernel, share, comps), grid=(group...  7.09 us
    all_to_all x1, waiting for transfers between devices, per_device(): both = lax.all_to_all(terms, 'gene', 0, 0)  3.99 us
    all_to_all x1, starting transfers between devices, per_device(): lax.all_to_all(jnp.broadcast_to(message[None], (groups,) + message.shape)...  3.52 us
  transfers between devices with their start and end apart: 9, of which 5 were waited for; matrix products, arithmetic and copies ran while one was open for 10% of the time, Pallas kernels for 0%

profile of v2, /device:TPU:1, one launch (start us, length us, event | category | flops | bytes accessed | tf_op | source)
XLA Modules:
  0.0 105.0 jit_solution(17510916409361405520)
XLA Ops:
  0.6 0.0 copy-start
  0.7 1.0 copy-done
  1.7 0.0 copy-start.3
  1.7 1.4 %fusion.3 = f16[256,256]{1,0:T(8,128)(2,1)S(1)} fusion(bf16[1024,256]{1,0:T(8,128)(2,1)S(1)} %copy-done, bf16[2048,1024]{1,0:T(8,128)(2,1)} %param.30, s32[]{:T(128)S(6)} %select_n.56), kind=kOutput, calls=%fused_computation.7 | convolution fusion | flops 134348800 | bytes 1179652 | tf_op jit(solution)/shard_map/dot_general | solution.py:117
  3.1 1.4 %fusion.2 = f16[256,256]{1,0:T(8,128)(2,1)S(1)} fusion(bf16[1024,256]{1,0:T(8,128)(2,1)S(1)} %copy-done, bf16[2048,1024]{1,0:T(8,128)(2,1)} %param.30, s32[]{:T(128)S(6)} %select_n.55), kind=kOutput, calls=%fused_computation.6 | convolution fusion | flops 134348800 | bytes 1179652 | tf_op jit(solution)/shard_map/dot_general | solution.py:117
  4.4 0.1 pad_maximum_fusion.1
  4.5 4.4 %collective-permute-start.24 = (f16[512,256]{1,0:T(8,128)(2,1)S(1)}, f16[512,256]{1,0:T(8,128)(2,1)S(1)}, u32[]{:S(2)}, u32[]{:S(2)}) collective-permute-start(f16[512,256]{1,0:T(8,128)(2,1)S(1)} %pad_maximum_fusion.1), channel_id=1, source_target_pairs={{0,1},{1,0},{2,3},{3,2},{4,5},{5,4},{6,7},{7,6},{8,9},{9,8},{10,11... | collective-permute-start | bytes 786440 | tf_op jit(solution)/shard_map/ppermute | solution.py:17
  8.9 1.4 %fusion.1 = f16[256,256]{1,0:T(8,128)(2,1)S(1)} fusion(bf16[1024,256]{1,0:T(8,128)(2,1)S(1)} %copy-done, bf16[2048,1024]{1,0:T(8,128)(2,1)} %param.30, s32[]{:T(128)S(6)} %select_n.52), kind=kOutput, calls=%fused_computation.5 | convolution fusion | flops 134348800 | bytes 1179652 | tf_op jit(solution)/shard_map/dot_general | solution.py:117
  10.3 1.4 %fusion = f16[256,256]{1,0:T(8,128)(2,1)S(1)} fusion(bf16[1024,256]{1,0:T(8,128)(2,1)S(1)} %copy-done, bf16[2048,1024]{1,0:T(8,128)(2,1)} %param.30, s32[]{:T(128)S(6)} %select_n.51), kind=kOutput, calls=%fused_computation.4 | convolution fusion | flops 134348800 | bytes 1179652 | tf_op jit(solution)/shard_map/dot_general | solution.py:117
  11.6 0.1 pad_maximum_fusion
  11.7 1.9 %collective-permute-start.22 = (f16[512,256]{1,0:T(8,128)(2,1)S(1)}, f16[512,256]{1,0:T(8,128)(2,1)S(1)}, u32[]{:S(2)}, u32[]{:S(2)}) collective-permute-start(f16[512,256]{1,0:T(8,128)(2,1)S(1)} %pad_maximum_fusion), channel_id=1, source_target_pairs={{0,1},{1,0},{2,3},{3,2},{4,5},{5,4},{6,7},{7,6},{8,9},{9,8},{10,11... | collective-permute-start | bytes 786440 | tf_op jit(solution)/shard_map/ppermute | solution.py:17
  13.6 1.3 %fusion.9 = f32[256,256]{1,0:T(8,128)S(1)} fusion(bf16[1024,256]{1,0:T(8,128)(2,1)S(1)} %copy-done, bf16[2048,1024]{1,0:T(8,128)(2,1)} %param.30, s32[]{:T(128)S(6)} %select_n.54), kind=kOutput, calls=%fused_computation.14 | convolution fusion | flops 134217728 | bytes 1310724 | tf_op jit(solution)/shard_map/dot_general | solution.py:117
  15.0 1.3 %fusion.15 = f32[256,256]{1,0:T(8,128)S(1)} fusion(bf16[1024,256]{1,0:T(8,128)(2,1)S(1)} %copy-done, bf16[2048,1024]{1,0:T(8,128)(2,1)} %param.30, s32[]{:T(128)S(6)} %select_n.50), kind=kOutput, calls=%fused_computation.20 | convolution fusion | flops 134217728 | bytes 1310724 | tf_op jit(solution)/shard_map/dot_general | solution.py:117
  16.4 0.0 copy-done.3
  16.4 0.0 copy-start.4
  16.4 0.0 collective-permute-done.24
  16.4 1.4 %reduce-precision_convert_fusion = f16[256,256]{1,0:T(8,128)(2,1)S(1)} fusion(f16[512,256]{1,0:T(8,128)(2,1)S(1)} %collective-permute-done.24, bf16[1024,256]{1,0:T(8,128)(2,1)S(1)} %copy-done, bf16[2048,1024]{1,0:T(8,128)(2,1)} %param.30, s32[]{:T(128)S(6)} %select_n.57), kind=kOutput, calls=%fused_computation.27 | convolution fusion | flops 134479872 | bytes 1310724 | tf_op jit(solution)/shard_map/dot_general | solution.py:117
  17.8 4.9 %collective-permute-start.25 = (f16[256,256]{1,0:T(8,128)(2,1)S(1)}, f16[256,256]{1,0:T(8,128)(2,1)S(1)}, u32[]{:S(2)}, u32[]{:S(2)}) collective-permute-start(f16[256,256]{1,0:T(8,128)(2,1)S(1)} %reduce-precision_convert_fusion), channel_id=1, source_target_pairs={{0,2},{1,3},{2,0},{3,1},{4,6},{5,7},{6,4},{7,5},{8,10},{9,11},{10,... | collective-permute-start | bytes 393224 | tf_op jit(solution)/shard_map/ppermute | solution.py:17
  22.7 0.0 collective-permute-done.22
  22.7 1.4 %reduce-precision_convert_fusion.1 = f16[256,256]{1,0:T(8,128)(2,1)S(1)} fusion(f16[512,256]{1,0:T(8,128)(2,1)S(1)} %collective-permute-done.22, bf16[1024,256]{1,0:T(8,128)(2,1)S(1)} %copy-done, bf16[2048,1024]{1,0:T(8,128)(2,1)} %param.30, s32[]{:T(128)S(6)} %select_n.53), kind=kOutput, calls=%fused_computation.29 | convolution fusion | flops 134479872 | bytes 1310724 | tf_op jit(solution)/shard_map/dot_general | solution.py:117
  24.1 2.6 %collective-permute-start.23 = (f16[256,256]{1,0:T(8,128)(2,1)S(1)}, f16[256,256]{1,0:T(8,128)(2,1)S(1)}, u32[]{:S(2)}, u32[]{:S(2)}) collective-permute-start(f16[256,256]{1,0:T(8,128)(2,1)S(1)} %reduce-precision_convert_fusion.1), channel_id=1, source_target_pairs={{0,2},{1,3},{2,0},{3,1},{4,6},{5,7},{6,4},{7,5},{8,10},{9,11},{10,... | collective-permute-start | bytes 393224 | tf_op jit(solution)/shard_map/ppermute | solution.py:17
  26.8 0.0 collective-permute-done.25
  26.8 0.1 add_convert_fusion
  26.8 9.7 %collective-permute-done.23 = f16[256,256]{1,0:T(8,128)(2,1)S(1)} collective-permute-done((f16[256,256]{1,0:T(8,128)(2,1)S(1)}, f16[256,256]{1,0:T(8,128)(2,1)S(1)}, u32[]{:S(2)}, u32[]{:S(2)}) %collective-permute-start.23) | collective-permute-done | bytes 131104 | tf_op jit(solution)/shard_map/ppermute | solution.py:17
  36.5 0.1 add_convert_fusion.1
  36.6 0.0 copy-start.1
  36.6 0.0 copy-start.2
  36.6 1.1 %broadcast_in_dim.11 = bf16[4,528,256]{2,1,0:T(8,128)(2,1)} broadcast(bf16[528,256]{1,0:T(8,128)(2,1)S(1)} %fusion.17), dimensions={1,2} | broadcast | bytes 1351680 | tf_op jit(solution)/shard_map/broadcast_in_dim | solution.py:133
  37.7 3.5 %all-to-all-start = ((bf16[4,528,256]{2,1,0:T(8,128)(2,1)}), bf16[4,528,256]{2,1,0:T(8,128)(2,1)S(1)}, u32[]{:S(2)}, u32[]{:S(2)}) async-start(bf16[4,528,256]{2,1,0:T(8,128)(2,1)} %broadcast_in_dim.11), calls=%async_computation | async-start | bytes 2162688 | tf_op jit(solution)/shard_map/all_to_all | solution.py:133
  41.2 15.2 %collective-permute-start.26 = (bf16[512,256]{1,0:T(8,128)(2,1)S(1)}, bf16[512,256]{1,0:T(8,128)(2,1)S(1)}, u32[]{:S(2)}, u32[]{:S(2)}) collective-permute-start(bf16[512,256]{1,0:T(8,128)(2,1)S(1)} %pad_maximum_fusion.2.own_ref), channel_id=1, source_target_pairs={{0,508},{4,504},{8,500},{12,496},{16,492},{20,488},{24,484},{28,48... | collective-permute-start | bytes 786440 | tf_op jit(solution)/shard_map/ppermute | solution.py:17
  56.5 0.0 copy-done.4
  56.5 0.6 fusion.30
  59.0 0.1 pad_add_fusion.where_ref
  59.1 11.7 %conditional.2 = (bf16[512,256]{1,0:T(8,128)(2,1)}) conditional(s32[]{:T(128)} %clamp.7, bf16[512,256]{1,0:T(8,128)(2,1)S(1)} %pad_maximum_fusion.2.own_ref, bf16[512,256]{1,0:T(8,128)(2,1)S(1)} %pad_maximum_fusion.2.own_ref, bf16[512,256]{1,0:T(8,128)(2,1)S(1)} %pad_maximum_fusion.2.own_ref, ...), branch_computations={%region_0.1_spmd, %region_1.2_spmd, %region_2.3_spmd, %region_3.4_... | conditional | bytes 1048624 | solution.py:24
  59.1 2.2 %collective-permute-start.7 = (bf16[512,256]{1,0:T(8,128)(2,1)S(1)}, bf16[512,256]{1,0:T(8,128)(2,1)}, u32[]{:S(2)}, u32[]{:S(2)}) collective-permute-start(bf16[512,256]{1,0:T(8,128)(2,1)S(1)} %param.8), channel_id=1, source_target_pairs={{0,256},{4,260},{8,264},{12,268},{16,272},{20,276},{24,280},{28,28... | collective-permute-start | bytes 786440 | tf_op jit(solution)/shard_map/cond/branch_8_fun/ppermute | solution.py:17
  61.4 9.5 %collective-permute-done.7 = bf16[512,256]{1,0:T(8,128)(2,1)} collective-permute-done((bf16[512,256]{1,0:T(8,128)(2,1)S(1)}, bf16[512,256]{1,0:T(8,128)(2,1)}, u32[]{:S(2)}, u32[]{:S(2)}) %collective-permute-start.7) | collective-permute-done | bytes 262176 | tf_op jit(solution)/shard_map/cond/branch_8_fun/ppermute | solution.py:17
  70.8 4.3 %conditional.3 = (bf16[512,256]{1,0:T(8,128)(2,1)}) conditional(s32[]{:T(128)} %clamp.6, bf16[512,256]{1,0:T(8,128)(2,1)} %get-tuple-element.58, bf16[512,256]{1,0:T(8,128)(2,1)} %get-tuple-element.58, bf16[512,256]{1,0:T(8,128)(2,1)} %get-tuple-element.58, bf16[512,256]{1,0:T(8,128)(2,1)} %get-tuple-element.58, ...), branch_computations={%region_16.17_spmd, %region_17.18_spmd, %region_18.19_spmd, %regio... | conditional | bytes 1572912 | solution.py:24
  70.8 2.3 %collective-permute-start.15 = (bf16[512,256]{1,0:T(8,128)(2,1)}, bf16[512,256]{1,0:T(8,128)(2,1)S(1)}, u32[]{:S(2)}, u32[]{:S(2)}) collective-permute-start(bf16[512,256]{1,0:T(8,128)(2,1)} %param.17), channel_id=1, source_target_pairs={{0,4},{4,0},{8,12},{12,8},{16,20},{20,16},{24,28},{28,24},{32,36},... | collective-permute-start | bytes 786440 | tf_op jit(solution)/shard_map/cond/branch_1_fun/ppermute | solution.py:17
  73.1 1.4 %collective-permute-done.15 = bf16[512,256]{1,0:T(8,128)(2,1)S(1)} collective-permute-done((bf16[512,256]{1,0:T(8,128)(2,1)}, bf16[512,256]{1,0:T(8,128)(2,1)S(1)}, u32[]{:S(2)}, u32[]{:S(2)}) %collective-permute-start.15) | collective-permute-done | bytes 262176 | tf_op jit(solution)/shard_map/cond/branch_1_fun/ppermute | solution.py:17
  74.5 0.7 copy.25
  75.2 2.8 %collective-permute-done.26.far_ref = bf16[512,256]{1,0:T(8,128)(2,1)S(1)} collective-permute-done((bf16[512,256]{1,0:T(8,128)(2,1)S(1)}, bf16[512,256]{1,0:T(8,128)(2,1)S(1)}, u32[]{:S(2)}, u32[]{:S(2)}) %collective-permute-start.26) | collective-permute-done | bytes 262176 | tf_op jit(solution)/shard_map/ppermute | solution.py:17
  78.0 0.0 all-to-all-done.query_ref
  78.0 0.0 copy-done.1
  78.0 0.0 copy-done.2
  78.0 7.1 %shard_map.77 = f32[4,2,512]{2,1,0:T(2,128)} custom-call(s32[4]{0:T(128)S(1)} %pad_add_fusion.where_ref, s32[128]{0:T(128)S(1)} %copy-done.2, f32[8]{0:T(128)S(1)} %copy-done.1, bf16[4,528,256]{2,1,0:T(8,128)(2,1)S(1)} %all-to-all-done.query_ref, bf16[512,256]{1,0:T(8,128)(2,1)S(1)} %pad_maximum_fusion.2.own_ref, ...), custom_call_target="tpu_custom_call" | custom-call | tf_op jit(solution)/shard_map/pallas_call | solution.py:86
  85.1 13.9 %all-to-all-start.1 = ((f32[4,2,512]{2,1,0:T(2,128)}), f32[4,2,512]{2,1,0:T(2,128)S(1)}, u32[]{:S(2)}, u32[]{:S(2)}) async-start(f32[4,2,512]{2,1,0:T(2,128)} %shard_map.77), calls=%async_computation.1 | async-start | bytes 32768 | tf_op jit(solution)/shard_map/all_to_all | solution.py:139
  99.0 0.6 dynamic_slice.27
  99.7 4.0 %all-to-all-done.1 = f32[4,2,512]{2,1,0:T(2,128)S(1)} async-done(((f32[4,2,512]{2,1,0:T(2,128)}), f32[4,2,512]{2,1,0:T(2,128)S(1)}, u32[]{:S(2)}, u32[]{:S(2)}) %all-to-all-start.1) | async-done | bytes 16416 | tf_op jit(solution)/shard_map/all_to_all | solution.py:139
  103.7 1.3 %sqrt_select_fusion = (f32[512]{0:T(512)}, f32[512]{0:T(512)}) fusion(f32[512]{0:T(512)S(1)} %get-tuple-element.52, s32[]{:T(128)} %bitcast, s32[]{:T(128)} %mul.8, f32[512]{0:T(512)S(1)} %get-tuple-element.53), kind=kLoop, calls=%fused_computation.32 | loop fusion | flops 2560 | bytes 8200 | tf_op jit(solution)/shard_map/jit(_where)/select_n | solution.py:144
  (5 shorter events, 0.1 us)
Async XLA Ops:
  0.6 1.0 copy-start
  1.7 14.7 %copy-start.3 = (s32[512]{0:T(512)S(1)}, s32[512]{0:T(512)}, u32[]{:S(2)}) copy-start(s32[512]{0:T(512)} %param.33) | copy-start | bytes 6148
  4.5 11.9 %collective-permute-start.24 = (f16[512,256]{1,0:T(8,128)(2,1)S(1)}, f16[512,256]{1,0:T(8,128)(2,1)S(1)}, u32[]{:S(2)}, u32[]{:S(2)}) collective-permute-start(f16[512,256]{1,0:T(8,128)(2,1)S(1)} %pad_maximum_fusion.1), channel_id=1, source_target_pairs={{0,1},{1,0},{2,3},{3,2},{4,5},{5,4},{6,7},{7,6},{8,9},{9,8},{10,11... | collective-permute-start | bytes 786440 | tf_op jit(solution)/shard_map/ppermute | solution.py:17
  11.7 11.0 %collective-permute-start.22 = (f16[512,256]{1,0:T(8,128)(2,1)S(1)}, f16[512,256]{1,0:T(8,128)(2,1)S(1)}, u32[]{:S(2)}, u32[]{:S(2)}) collective-permute-start(f16[512,256]{1,0:T(8,128)(2,1)S(1)} %pad_maximum_fusion), channel_id=1, source_target_pairs={{0,1},{1,0},{2,3},{3,2},{4,5},{5,4},{6,7},{7,6},{8,9},{9,8},{10,11... | collective-permute-start | bytes 786440 | tf_op jit(solution)/shard_map/ppermute | solution.py:17
  16.4 40.1 %copy-start.4 = (s32[2]{0:T(128)S(1)}, s32[2]{0:T(128)}, u32[]{:S(2)}) copy-start(s32[2]{0:T(128)} %param.35) | copy-start | bytes 28
  17.8 8.9 %collective-permute-start.25 = (f16[256,256]{1,0:T(8,128)(2,1)S(1)}, f16[256,256]{1,0:T(8,128)(2,1)S(1)}, u32[]{:S(2)}, u32[]{:S(2)}) collective-permute-start(f16[256,256]{1,0:T(8,128)(2,1)S(1)} %reduce-precision_convert_fusion), channel_id=1, source_target_pairs={{0,2},{1,3},{2,0},{3,1},{4,6},{5,7},{6,4},{7,5},{8,10},{9,11},{10,... | collective-permute-start | bytes 393224 | tf_op jit(solution)/shard_map/ppermute | solution.py:17
  24.1 12.4 %collective-permute-start.23 = (f16[256,256]{1,0:T(8,128)(2,1)S(1)}, f16[256,256]{1,0:T(8,128)(2,1)S(1)}, u32[]{:S(2)}, u32[]{:S(2)}) collective-permute-start(f16[256,256]{1,0:T(8,128)(2,1)S(1)} %reduce-precision_convert_fusion.1), channel_id=1, source_target_pairs={{0,2},{1,3},{2,0},{3,1},{4,6},{5,7},{6,4},{7,5},{8,10},{9,11},{10,... | collective-permute-start | bytes 393224 | tf_op jit(solution)/shard_map/ppermute | solution.py:17
  36.6 41.4 %copy-start.1 = (f32[8]{0:T(128)S(1)}, f32[8]{0:T(128)}, u32[]{:S(2)}) copy-start(f32[8]{0:T(128)} %widths_ref.1) | copy-start | bytes 100
  36.6 41.4 %copy-start.2 = (s32[128]{0:T(128)S(1)}, s32[128]{0:T(128)}, u32[]{:S(2)}) copy-start(s32[128]{0:T(128)} %fill_ref.1) | copy-start | bytes 1540
  37.7 40.3 %all-to-all-start = ((bf16[4,528,256]{2,1,0:T(8,128)(2,1)}), bf16[4,528,256]{2,1,0:T(8,128)(2,1)S(1)}, u32[]{:S(2)}, u32[]{:S(2)}) async-start(bf16[4,528,256]{2,1,0:T(8,128)(2,1)} %broadcast_in_dim.11), calls=%async_computation | async-start | bytes 2162688 | tf_op jit(solution)/shard_map/all_to_all | solution.py:133
  41.2 36.8 %collective-permute-start.26 = (bf16[512,256]{1,0:T(8,128)(2,1)S(1)}, bf16[512,256]{1,0:T(8,128)(2,1)S(1)}, u32[]{:S(2)}, u32[]{:S(2)}) collective-permute-start(bf16[512,256]{1,0:T(8,128)(2,1)S(1)} %pad_maximum_fusion.2.own_ref), channel_id=1, source_target_pairs={{0,508},{4,504},{8,500},{12,496},{16,492},{20,488},{24,484},{28,48... | collective-permute-start | bytes 786440 | tf_op jit(solution)/shard_map/ppermute | solution.py:17
  59.1 11.7 %collective-permute-start.7 = (bf16[512,256]{1,0:T(8,128)(2,1)S(1)}, bf16[512,256]{1,0:T(8,128)(2,1)}, u32[]{:S(2)}, u32[]{:S(2)}) collective-permute-start(bf16[512,256]{1,0:T(8,128)(2,1)S(1)} %param.8), channel_id=1, source_target_pairs={{0,256},{4,260},{8,264},{12,268},{16,272},{20,276},{24,280},{28,28... | collective-permute-start | bytes 786440 | tf_op jit(solution)/shard_map/cond/branch_8_fun/ppermute | solution.py:17
  70.8 3.6 %collective-permute-start.15 = (bf16[512,256]{1,0:T(8,128)(2,1)}, bf16[512,256]{1,0:T(8,128)(2,1)S(1)}, u32[]{:S(2)}, u32[]{:S(2)}) collective-permute-start(bf16[512,256]{1,0:T(8,128)(2,1)} %param.17), channel_id=1, source_target_pairs={{0,4},{4,0},{8,12},{12,8},{16,20},{20,16},{24,28},{28,24},{32,36},... | collective-permute-start | bytes 786440 | tf_op jit(solution)/shard_map/cond/branch_1_fun/ppermute | solution.py:17
  85.1 18.6 %all-to-all-start.1 = ((f32[4,2,512]{2,1,0:T(2,128)}), f32[4,2,512]{2,1,0:T(2,128)S(1)}, u32[]{:S(2)}, u32[]{:S(2)}) async-start(f32[4,2,512]{2,1,0:T(2,128)} %shard_map.77), calls=%async_computation.1 | async-start | bytes 32768 | tf_op jit(solution)/shard_map/all_to_all | solution.py:139

commit v3 on v2

v3 whole, which is shorter than its diff:
```python
import functools

import jax
import jax.numpy as jnp
from jax import lax
from jax.experimental import pallas as pl
from jax.experimental.pallas import tpu as pltpu
from jax.sharding import PartitionSpec as P

EXTRA = 16
BIG = 1e30
LOG2E = 1.4426950408889634


def swapped(value, axis, mask):
    pairs = [(source, source ^ mask) for source in range(lax.axis_size(axis))]
    return lax.ppermute(value, axis, pairs)


def chosen(value, axis, index, unit, count):
    moves = [lambda x: x]
    for step in range(1, count):
        moves.append(lambda x, mask=step * unit: swapped(x, axis, mask))
    return lax.switch(index, moves, value)


def squares(x):
    xf = x.astype(jnp.float32)
    square = xf * xf
    high = square.astype(jnp.bfloat16)
    low = (square - high.astype(jnp.float32)).astype(jnp.bfloat16)
    return high, low


def across(a, b):
    return lax.dot_general(a, b, (((1,), (1,)), ((), ())), preferred_element_type=jnp.float32)


def terms_kernel(share, comps, where_ref, fill_ref, widths_ref, mine_ref, second_ref, beside_ref, across_ref, own_ref, far_ref, other_ref, out_ref, near_ref, wide_ref, twice_ref):
    first = where_ref[0] * share
    keys = (own_ref, far_ref, other_ref)
    ones = jnp.ones((128, comps), jnp.bfloat16)
    slot = first + lax.broadcasted_iota(jnp.int32, (share, 128), 0)
    for n, key_ref in enumerate(keys):
        block = key_ref[...]
        high, low = squares(block)
        norm = across(high, ones) + across(low, ones)
        live = slot < fill_ref[where_ref[1 + n]]
        near_ref[n] = jnp.where(live, norm, BIG)
        wide_ref[n] = jnp.where(live, norm, -BIG)
        twice_ref[n] = block * jnp.bfloat16(-2)

    lanes = 256
    def step(query_ref, shard, begin):
        query = query_ref[pl.ds(begin, lanes), :]
        high, low = squares(query)
        few = jnp.ones((8, comps), jnp.bfloat16)
        norm = (across(few, high) + across(few, low))[:1]
        index = query_ref[share:, :].astype(jnp.float32)
        index = jnp.concatenate([index[row : row + 1] for row in range(begin // comps, (begin + lanes) // comps)], axis=1)
        width = jnp.zeros((1, lanes), jnp.float32)
        for n in range(widths_ref.shape[0]):
            width = jnp.where(index == float(n), widths_ref[n], width)
        coef = -LOG2E / (2.0 * comps * width * width)
        total = jnp.zeros((8, lanes), jnp.float32)
        top = jnp.full((8, lanes), -BIG, jnp.float32)
        for n in range(len(keys)):
            inner = across(twice_ref[n], query)
            near = jnp.concatenate([near_ref[n]] * (lanes // 128), axis=1)
            wide = jnp.concatenate([wide_ref[n]] * (lanes // 128), axis=1)
            dist = jnp.maximum(inner + near + norm, 0.0)
            kernel = jnp.exp2(dist * coef)
            total = total + jnp.sum(kernel.reshape(share // 8, 8, lanes), axis=0)
            top = jnp.maximum(top, jnp.max((inner + wide).reshape(share // 8, 8, lanes), axis=0))
        out_ref[shard, 0:1, pl.ds(begin, lanes)] = jnp.sum(total, axis=0, keepdims=True)
        out_ref[shard, 1:2, pl.ds(begin, lanes)] = jnp.maximum(jnp.max(top, axis=0, keepdims=True) + norm, 0.0)

    for ref, flip in ((mine_ref, 0), (second_ref, 2), (beside_ref, 1), (across_ref, 3)):
        shard = jnp.bitwise_xor(where_ref[0], flip)
        for begin in range(0, share, lanes):
            step(ref, shard, begin)


def block_terms(where, fill, widths, mine, beside, own, far, other):
    share, comps = own.shape
    groups = len(mine) + len(beside)
    whole = pl.BlockSpec(memory_space=pltpu.VMEM)
    smem = pl.BlockSpec(memory_space=pltpu.SMEM)
    return pl.pallas_call(
        functools.partial(terms_kernel, share, comps),
        out_shape=jax.ShapeDtypeStruct((groups, 2, share), jnp.float32),
        in_specs=[smem] * 3 + [whole] * 7,
        out_specs=whole,
        scratch_shapes=[
            pltpu.VMEM((3, share, 128), jnp.float32),
            pltpu.VMEM((3, share, 128), jnp.float32),
            pltpu.VMEM((3, share, comps), jnp.bfloat16),
        ],
        compiler_params=pltpu.CompilerParams(vmem_limit_bytes=32 * 1024 * 1024),
    )(where, fill, widths, *mine, *beside, own, far, other)


def per_device(counts, loadings, kernel_widths, width_index, block_fill, plan):
    groups = lax.axis_size("gene")
    blocks = lax.axis_size("cell")
    rows = counts.shape[0]
    share = rows // groups
    gene_pos = lax.axis_index("gene")
    cell_pos = lax.axis_index("cell")
    comps = loadings.shape[1]
    far = blocks - 1
    other = jnp.where(plan[0] == far, plan[1], plan[0])
    where = jnp.stack([gene_pos, cell_pos, jnp.bitwise_xor(cell_pos, far), jnp.bitwise_xor(cell_pos, other)])
    first = gene_pos * share
    forward = jnp.bitwise_and(other, 4) != 0
    path = jnp.where(forward, jnp.bitwise_xor(other, far), other)
    early = jnp.where(forward, 0, path % 4)
    late = jnp.where(forward, path % 4, 0)
    across_plane = path // 8
    index = jnp.pad(width_index.reshape(-1, comps), ((0, EXTRA - share // comps), (0, 0)))

    chunks = 2
    half = share // chunks

    def partial(shard, chunk):
        begin = jnp.bitwise_xor(gene_pos, shard) * share + chunk * half
        rows = lax.dynamic_slice_in_dim(counts, begin, half, 0)
        return jnp.dot(rows, loadings, preferred_element_type=jnp.float32)

    def narrow(x):
        return lax.reduce_precision(x, 8, 10).astype(jnp.float16)

    def widen(x):
        return x.astype(jnp.float32)

    near = [swapped(jnp.concatenate([narrow(partial(1, c)), narrow(partial(3, c))]), "gene", 1) for c in range(chunks)]
    pair = [
        (narrow(partial(0, c) + widen(near[c][:half])), narrow(partial(2, c) + widen(near[c][half:])))
        for c in range(chunks)
    ]
    wide = [swapped(pair[c][1], "gene", 2) for c in range(chunks)]
    back = swapped(jnp.concatenate([pair[c][0] for c in range(chunks)] + [index.astype(jnp.float16)]), "gene", 2)
    wide[0], forward, early, late, across_plane, where = lax.optimization_barrier((wide[0], forward, early, late, across_plane, where))
    scores = jnp.concatenate([widen(pair[c][0]) + widen(wide[c]) for c in range(chunks)]).astype(jnp.bfloat16)
    partner = swapped(scores, "cell", far)
    moved = chosen(scores, "cell", early, 1, 4)
    back, moved = lax.optimization_barrier((back, moved))
    second = jnp.concatenate([widen(pair[c][1]) + widen(back[c * half : (c + 1) * half]) for c in range(chunks)]).astype(jnp.bfloat16)
    mine = [
        jnp.concatenate([scores, index.astype(jnp.bfloat16)]),
        jnp.concatenate([second, back[share:].astype(jnp.bfloat16)]),
    ]
    beside = [swapped(part, "gene", 1) for part in mine]
    moved = jnp.where(forward, partner, moved)
    moved = chosen(moved, "cell", late, 1, 4)
    moved = chosen(moved, "cell", across_plane, 8, blocks // 8)

    terms = block_terms(where, block_fill, kernel_widths, mine, beside, scores, partner, moved)
    both = lax.all_to_all(terms, "gene", 0, 0)
    total = jnp.sum(both[:, 0], axis=0)
    top = jnp.max(both[:, 1], axis=0)
    qlive = first + jnp.arange(share, dtype=jnp.int32) < block_fill[cell_pos]
    density = jnp.where(qlive, jnp.log(total), 0.0)
    spread = jnp.where(qlive, jnp.sqrt(top / comps), 0.0)
    return (density, spread)


def solution(mesh):
    placed = (P("cell", "gene"), P("gene", None), P(), P(("cell", "gene")), P(), P())
    return jax.shard_map(
        per_device,
        mesh=mesh,
        in_specs=placed,
        out_specs=(P(("cell", "gene")), P(("cell", "gene"))),
        check_vma=False,
    )
```

time: 106 us -> 117 us (1.10)
  waiting for transfers between devices: 27.3 us -> 34.4 us
  starting transfers between devices: 51 us -> 56.9 us
  local copies, waits for them, and re-layouts: 4.04 us -> 2.24 us
  Pallas kernels: 7.09 us -> 5.64 us
    ppermute x7 -> x10, starting transfers between devices: 33.6 us -> 53.6 us  [swapped(): return lax.ppermute(value, axis, pairs)]
    all_to_all x1, starting transfers between devices: 13.9 us -> 3.24 us  [per_device(): both = lax.all_to_all(terms, 'gene', 0, 0)]
    ppermute x7 -> x10, waiting for transfers between devices: 23.3 us -> 30.6 us  [swapped(): return lax.ppermute(value, axis, pairs)]
    all_to_all x1 -> x0, starting transfers between devices: 3.52 us -> none  [per_device(): lax.all_to_all(jnp.broadcast_to(message[None], (groups,) + message.shape)...]
    pallas_call x1, Pallas kernels: 7.09 us -> 5.64 us  [block_terms(): pl.pallas_call(functools.partial(terms_kernel, share, comps), out_shape=j...]
  transfers between devices with their start and end apart: 9 -> 11, of which waited for: 5 -> 4; matrix products, arithmetic and copies ran while one was open for 10% -> 9% of each run, Pallas kernels for 0% -> 0%
where the time goes in v3:
time: 117 us; the launch traced here: 116 us
  starting transfers between devices  56.9 us (49%)
  waiting for transfers between devices  34.4 us (29%)
  matrix products  11 us (9%)
  Pallas kernels  5.64 us (5%)
  between operations  2.92 us (2%)
  other arithmetic  2.74 us (2%)
  local copies, waits for them, and re-layouts  2.24 us (2%)
    ppermute x10, starting transfers between devices, swapped(): return lax.ppermute(value, axis, pairs)  53.6 us
    ppermute x10, waiting for transfers between devices, swapped(): return lax.ppermute(value, axis, pairs)  30.6 us
    dot_general x8, matrix products, partial(): return jnp.dot(rows, loadings, preferred_element_type=jnp.float32)  11 us
    pallas_call x1, Pallas kernels, block_terms(): pl.pallas_call(functools.partial(terms_kernel, share, comps), out_shape=j...  5.64 us
    all_to_all x1, waiting for transfers between devices, per_device(): both = lax.all_to_all(terms, 'gene', 0, 0)  3.83 us
    all_to_all x1, starting transfers between devices, per_device(): both = lax.all_to_all(terms, 'gene', 0, 0)  3.24 us
  transfers between devices with their start and end apart: 11, of which 4 were waited for; matrix products, arithmetic and copies ran while one was open for 9% of the time, Pallas kernels for 0%

profile of v3, /device:TPU:1, one launch (start us, length us, event | category | flops | bytes accessed | tf_op | source)
XLA Modules:
  0.0 116.0 jit_solution(14200322545141587721)
XLA Ops:
  0.6 0.0 copy-start
  0.6 0.0 copy-start.4
  0.7 0.0 copy-start.3
  0.7 1.0 copy-done
  1.7 1.4 %fusion.2 = f16[256,256]{1,0:T(8,128)(2,1)S(1)} fusion(bf16[1024,256]{1,0:T(8,128)(2,1)S(1)} %copy-done, bf16[2048,1024]{1,0:T(8,128)(2,1)} %param.30, s32[]{:T(128)S(6)} %select_n.85), kind=kOutput, calls=%fused_computation.6 | convolution fusion | flops 134348800 | bytes 1179652 | tf_op jit(solution)/shard_map/dot_general | solution.py:128
  3.0 1.4 %fusion.3 = f16[256,256]{1,0:T(8,128)(2,1)S(1)} fusion(bf16[1024,256]{1,0:T(8,128)(2,1)S(1)} %copy-done, bf16[2048,1024]{1,0:T(8,128)(2,1)} %param.30, s32[]{:T(128)S(6)} %select_n.86), kind=kOutput, calls=%fused_computation.7 | convolution fusion | flops 134348800 | bytes 1179652 | tf_op jit(solution)/shard_map/dot_general | solution.py:128
  4.4 0.1 pad_maximum_fusion.4
  4.5 4.4 %collective-permute-start.23 = (f16[512,256]{1,0:T(8,128)(2,1)S(1)}, f16[512,256]{1,0:T(8,128)(2,1)S(1)}, u32[]{:S(2)}, u32[]{:S(2)}) collective-permute-start(f16[512,256]{1,0:T(8,128)(2,1)S(1)} %pad_maximum_fusion.4), channel_id=1, source_target_pairs={{0,1},{1,0},{2,3},{3,2},{4,5},{5,4},{6,7},{7,6},{8,9},{9,8},{10,11... | collective-permute-start | bytes 786440 | tf_op jit(solution)/shard_map/ppermute | solution.py:17
  8.9 1.4 %fusion = f16[256,256]{1,0:T(8,128)(2,1)S(1)} fusion(bf16[1024,256]{1,0:T(8,128)(2,1)S(1)} %copy-done, bf16[2048,1024]{1,0:T(8,128)(2,1)} %param.30, s32[]{:T(128)S(6)} %select_n.75), kind=kOutput, calls=%fused_computation.4 | convolution fusion | flops 134348800 | bytes 1179652 | tf_op jit(solution)/shard_map/dot_general | solution.py:128
  10.3 1.4 %fusion.1 = f16[256,256]{1,0:T(8,128)(2,1)S(1)} fusion(bf16[1024,256]{1,0:T(8,128)(2,1)S(1)} %copy-done, bf16[2048,1024]{1,0:T(8,128)(2,1)} %param.30, s32[]{:T(128)S(6)} %select_n.76), kind=kOutput, calls=%fused_computation.5 | convolution fusion | flops 134348800 | bytes 1179652 | tf_op jit(solution)/shard_map/dot_general | solution.py:128
  11.6 0.1 pad_maximum_fusion.3
  11.7 1.9 %collective-permute-start.21 = (f16[512,256]{1,0:T(8,128)(2,1)S(1)}, f16[512,256]{1,0:T(8,128)(2,1)S(1)}, u32[]{:S(2)}, u32[]{:S(2)}) collective-permute-start(f16[512,256]{1,0:T(8,128)(2,1)S(1)} %pad_maximum_fusion.3), channel_id=1, source_target_pairs={{0,1},{1,0},{2,3},{3,2},{4,5},{5,4},{6,7},{7,6},{8,9},{9,8},{10,11... | collective-permute-start | bytes 786440 | tf_op jit(solution)/shard_map/ppermute | solution.py:17
  13.6 0.0 copy-done.4
  13.6 0.6 fusion.32
  16.1 0.0 copy-done.3
  16.2 0.1 pad_add_fusion.where_ref
  16.2 0.0 collective-permute-done.23
  16.2 1.4 %reduce-precision_convert_fusion = f16[256,256]{1,0:T(8,128)(2,1)S(1)} fusion(f16[512,256]{1,0:T(8,128)(2,1)S(1)} %collective-permute-done.23, bf16[1024,256]{1,0:T(8,128)(2,1)S(1)} %copy-done, bf16[2048,1024]{1,0:T(8,128)(2,1)} %param.30, s32[]{:T(128)S(6)} %select_n.87), kind=kOutput, calls=%fused_computation.29 | convolution fusion | flops 134479872 | bytes 1310724 | tf_op jit(solution)/shard_map/dot_general | solution.py:128
  17.6 4.9 %collective-permute-start.24 = (f16[256,256]{1,0:T(8,128)(2,1)S(1)}, f16[256,256]{1,0:T(8,128)(2,1)S(1)}, u32[]{:S(2)}, u32[]{:S(2)}) collective-permute-start(f16[256,256]{1,0:T(8,128)(2,1)S(1)} %reduce-precision_convert_fusion), channel_id=1, source_target_pairs={{0,2},{1,3},{2,0},{3,1},{4,6},{5,7},{6,4},{7,5},{8,10},{9,11},{10,... | collective-permute-start | bytes 393224 | tf_op jit(solution)/shard_map/ppermute | solution.py:17
  22.5 0.0 collective-permute-done.21
  22.6 1.4 %reduce-precision_convert_fusion.3 = f16[256,256]{1,0:T(8,128)(2,1)S(1)} fusion(f16[512,256]{1,0:T(8,128)(2,1)S(1)} %collective-permute-done.21, bf16[1024,256]{1,0:T(8,128)(2,1)S(1)} %copy-done, bf16[2048,1024]{1,0:T(8,128)(2,1)} %param.30, s32[]{:T(128)S(6)} %select_n.74), kind=kOutput, calls=%fused_computation.33 | convolution fusion | flops 134479872 | bytes 1310724 | tf_op jit(solution)/shard_map/dot_general | solution.py:128
  23.9 2.8 %collective-permute-start.22 = (f16[256,256]{1,0:T(8,128)(2,1)S(1)}, f16[256,256]{1,0:T(8,128)(2,1)S(1)}, u32[]{:S(2)}, u32[]{:S(2)}) collective-permute-start(f16[256,256]{1,0:T(8,128)(2,1)S(1)} %reduce-precision_convert_fusion.3), channel_id=1, source_target_pairs={{0,2},{1,3},{2,0},{3,1},{4,6},{5,7},{6,4},{7,5},{8,10},{9,11},{10,... | collective-permute-start | bytes 393224 | tf_op jit(solution)/shard_map/ppermute | solution.py:17
  26.7 1.4 %reduce-precision_convert_fusion.1 = f16[256,256]{1,0:T(8,128)(2,1)S(1)} fusion(f16[512,256]{1,0:T(8,128)(2,1)S(1)} %collective-permute-done.23, bf16[1024,256]{1,0:T(8,128)(2,1)S(1)} %copy-done, bf16[2048,1024]{1,0:T(8,128)(2,1)} %param.30, s32[]{:T(128)S(6)} %select_n.84), kind=kOutput, calls=%fused_computation.30 | convolution fusion | flops 134479872 | bytes 1310724 | tf_op jit(solution)/shard_map/dot_general | solution.py:128
  28.1 1.4 %reduce-precision_convert_fusion.2 = f16[256,256]{1,0:T(8,128)(2,1)S(1)} fusion(f16[512,256]{1,0:T(8,128)(2,1)S(1)} %collective-permute-done.21, bf16[1024,256]{1,0:T(8,128)(2,1)S(1)} %copy-done, bf16[2048,1024]{1,0:T(8,128)(2,1)} %param.30, s32[]{:T(128)S(6)} %select_n.83), kind=kOutput, calls=%fused_computation.32 | convolution fusion | flops 134479872 | bytes 1310724 | tf_op jit(solution)/shard_map/dot_general | solution.py:128
  29.5 0.1 pad_maximum_fusion.1
  29.6 3.4 %collective-permute-start.25 = (f16[528,256]{1,0:T(8,128)(2,1)S(1)}, f16[528,256]{1,0:T(8,128)(2,1)S(1)}, u32[]{:S(2)}, u32[]{:S(2)}) collective-permute-start(f16[528,256]{1,0:T(8,128)(2,1)S(1)} %pad_maximum_fusion.1), channel_id=1, source_target_pairs={{0,2},{1,3},{2,0},{3,1},{4,6},{5,7},{6,4},{7,5},{8,10},{9,11},{10,... | collective-permute-start | bytes 811016 | tf_op jit(solution)/shard_map/ppermute | solution.py:17
  33.0 3.3 %collective-permute-done.22 = f16[256,256]{1,0:T(8,128)(2,1)S(1)} collective-permute-done((f16[256,256]{1,0:T(8,128)(2,1)S(1)}, f16[256,256]{1,0:T(8,128)(2,1)S(1)}, u32[]{:S(2)}, u32[]{:S(2)}) %collective-permute-start.22) | collective-permute-done | bytes 131104 | tf_op jit(solution)/shard_map/ppermute | solution.py:17
  36.4 0.0 collective-permute-done.24
  36.5 21.6 %collective-permute-start.28 = (bf16[512,256]{1,0:T(8,128)(2,1)S(1)}, bf16[512,256]{1,0:T(8,128)(2,1)S(1)}, u32[]{:S(2)}, u32[]{:S(2)}) collective-permute-start(bf16[512,256]{1,0:T(8,128)(2,1)S(1)} %pad_maximum_fusion.5.own_ref), channel_id=1, source_target_pairs={{0,508},{4,504},{8,500},{12,496},{16,492},{20,488},{24,484},{28,48... | collective-permute-start | bytes 786440 | tf_op jit(solution)/shard_map/ppermute | solution.py:17
  58.1 23.5 %conditional.3 = (bf16[512,256]{1,0:T(8,128)(2,1)}) conditional(s32[]{:T(128)} %clamp.9, bf16[512,256]{1,0:T(8,128)(2,1)S(1)} %pad_maximum_fusion.5.own_ref, bf16[512,256]{1,0:T(8,128)(2,1)S(1)} %pad_maximum_fusion.5.own_ref, bf16[512,256]{1,0:T(8,128)(2,1)S(1)} %pad_maximum_fusion.5.own_ref, ...), branch_computations={%region_0.1_spmd, %region_1.2_spmd, %region_2.3_spmd, %region_3.4_... | conditional | bytes 1048624 | solution.py:24
  58.1 5.2 %collective-permute-start.1 = (bf16[512,256]{1,0:T(8,128)(2,1)S(1)}, bf16[512,256]{1,0:T(8,128)(2,1)}, u32[]{:S(2)}, u32[]{:S(2)}) collective-permute-start(bf16[512,256]{1,0:T(8,128)(2,1)S(1)} %param.2), channel_id=1, source_target_pairs={{0,8},{4,12},{8,0},{12,4},{16,24},{20,28},{24,16},{28,20},{32,40},... | collective-permute-start | bytes 786440 | tf_op jit(solution)/shard_map/cond/branch_2_fun/ppermute | solution.py:17
  63.3 18.3 %collective-permute-done.1 = bf16[512,256]{1,0:T(8,128)(2,1)} collective-permute-done((bf16[512,256]{1,0:T(8,128)(2,1)S(1)}, bf16[512,256]{1,0:T(8,128)(2,1)}, u32[]{:S(2)}, u32[]{:S(2)}) %collective-permute-start.1) | collective-permute-done | bytes 262176 | tf_op jit(solution)/shard_map/cond/branch_2_fun/ppermute | solution.py:17
  81.6 1.9 %collective-permute-start.26 = (bf16[528,256]{1,0:T(8,128)(2,1)S(1)}, bf16[528,256]{1,0:T(8,128)(2,1)S(1)}, u32[]{:S(2)}, u32[]{:S(2)}) collective-permute-start(bf16[528,256]{1,0:T(8,128)(2,1)S(1)} %pad_maximum_fusion.mine_ref), channel_id=1, source_target_pairs={{0,1},{1,0},{2,3},{3,2},{4,5},{5,4},{6,7},{7,6},{8,9},{9,8},{10,11... | collective-permute-start | bytes 811016 | tf_op jit(solution)/shard_map/ppermute | solution.py:17
  83.5 0.0 collective-permute-done.25
  83.5 0.1 add_convert_fusion.1
  83.7 3.4 %collective-permute-start.27 = (bf16[528,256]{1,0:T(8,128)(2,1)S(1)}, bf16[528,256]{1,0:T(8,128)(2,1)S(1)}, u32[]{:S(2)}, u32[]{:S(2)}) collective-permute-start(bf16[528,256]{1,0:T(8,128)(2,1)S(1)} %pad_maximum_fusion.2.second_ref), channel_id=1, source_target_pairs={{0,1},{1,0},{2,3},{3,2},{4,5},{5,4},{6,7},{7,6},{8,9},{9,8},{10,11... | collective-permute-start | bytes 811016 | tf_op jit(solution)/shard_map/ppermute | solution.py:17
  87.0 0.0 collective-permute-done.28.far_ref
  87.0 1.0 broadcast_select_fusion
  88.1 0.0 copy-start.1
  88.1 0.0 copy-start.2
  88.1 13.2 %conditional.5 = (bf16[512,256]{1,0:T(8,128)(2,1)S(1)}) conditional(s32[]{:T(128)} %clamp.10, bf16[512,256]{1,0:T(8,128)(2,1)S(1)} %get-tuple-element.80, bf16[512,256]{1,0:T(8,128)(2,1)S(1)} %get-tuple-element.80, bf16[512,256]{1,0:T(8,128)(2,1)S(1)} %get-tuple-element.80, ...), branch_computations={%region_8.9_spmd, %region_9.10_spmd, %region_10.11_spmd, %region_1... | conditional | bytes 1572912 | solution.py:24
  88.1 4.2 %collective-permute-start.15 = (bf16[512,256]{1,0:T(8,128)(2,1)S(1)}, bf16[512,256]{1,0:T(8,128)(2,1)S(1)}, u32[]{:S(2)}, u32[]{:S(2)}) collective-permute-start(bf16[512,256]{1,0:T(8,128)(2,1)S(1)} %param.18), channel_id=1, source_target_pairs={{0,320},{4,324},{8,328},{12,332},{16,336},{20,340},{24,344},{28,34... | collective-permute-start | bytes 786440 | tf_op jit(solution)/shard_map/cond/branch_10_fun/ppermute | solution.py:17
  92.3 9.0 %collective-permute-done.15 = bf16[512,256]{1,0:T(8,128)(2,1)S(1)} collective-permute-done((bf16[512,256]{1,0:T(8,128)(2,1)S(1)}, bf16[512,256]{1,0:T(8,128)(2,1)S(1)}, u32[]{:S(2)}, u32[]{:S(2)}) %collective-permute-start.15) | collective-permute-done | bytes 262176 | tf_op jit(solution)/shard_map/cond/branch_10_fun/ppermute | solution.py:17
  101.4 0.0 collective-permute-done.26.beside_ref
  101.4 0.0 collective-permute-done.27.across_ref
  101.4 0.0 copy-done.1
  101.4 0.0 copy-done.2
  101.4 5.6 %shard_map.77 = f32[4,2,512]{2,1,0:T(2,128)} custom-call(s32[4]{0:T(128)S(1)} %pad_add_fusion.where_ref, s32[128]{0:T(128)S(1)} %copy-done.2, f32[8]{0:T(128)S(1)} %copy-done.1, bf16[528,256]{1,0:T(8,128)(2,1)S(1)} %pad_maximum_fusion.mine_ref, bf16[528,256]{1,0:T(8,128)(2,1)S(1)} %pad_maximum_fusion.2.second_ref, ...), custom_call_target="tpu_custom_call" | custom-call | tf_op jit(solution)/shard_map/pallas_call | solution.py:89
  107.0 3.2 %all-to-all-start = ((f32[4,2,512]{2,1,0:T(2,128)}), f32[4,2,512]{2,1,0:T(2,128)S(1)}, u32[]{:S(2)}, u32[]{:S(2)}) async-start(f32[4,2,512]{2,1,0:T(2,128)} %shard_map.77), calls=%async_computation | async-start | bytes 32768 | tf_op jit(solution)/shard_map/all_to_all | solution.py:159
  110.3 0.6 dynamic_slice.27
  110.9 3.8 %all-to-all-done = f32[4,2,512]{2,1,0:T(2,128)S(1)} async-done(((f32[4,2,512]{2,1,0:T(2,128)}), f32[4,2,512]{2,1,0:T(2,128)S(1)}, u32[]{:S(2)}, u32[]{:S(2)}) %all-to-all-start) | async-done | bytes 16416 | tf_op jit(solution)/shard_map/all_to_all | solution.py:159
  114.7 1.2 %sqrt_select_fusion = (f32[512]{0:T(512)}, f32[512]{0:T(512)}) fusion(f32[512]{0:T(512)S(1)} %get-tuple-element.69, s32[]{:T(128)} %bitcast, s32[]{:T(128)S(6)} %mul.8, f32[512]{0:T(512)S(1)} %get-tuple-element.70), kind=kLoop, calls=%fused_computation.40 | loop fusion | flops 2560 | bytes 8200 | tf_op jit(solution)/shard_map/jit(_where)/select_n | solution.py:164
  (11 shorter events, 0.2 us)
Async XLA Ops:
  0.6 1.0 copy-start
  0.6 13.0 %copy-start.4 = (s32[2]{0:T(128)S(1)}, s32[2]{0:T(128)}, u32[]{:S(2)}) copy-start(s32[2]{0:T(128)} %param.35) | copy-start | bytes 28
  0.7 15.5 %copy-start.3 = (s32[512]{0:T(512)S(1)}, s32[512]{0:T(512)}, u32[]{:S(2)}) copy-start(s32[512]{0:T(512)} %param.33) | copy-start | bytes 6148
  4.5 11.8 %collective-permute-start.23 = (f16[512,256]{1,0:T(8,128)(2,1)S(1)}, f16[512,256]{1,0:T(8,128)(2,1)S(1)}, u32[]{:S(2)}, u32[]{:S(2)}) collective-permute-start(f16[512,256]{1,0:T(8,128)(2,1)S(1)} %pad_maximum_fusion.4), channel_id=1, source_target_pairs={{0,1},{1,0},{2,3},{3,2},{4,5},{5,4},{6,7},{7,6},{8,9},{9,8},{10,11... | collective-permute-start | bytes 786440 | tf_op jit(solution)/shard_map/ppermute | solution.py:17
  11.7 10.8 %collective-permute-start.21 = (f16[512,256]{1,0:T(8,128)(2,1)S(1)}, f16[512,256]{1,0:T(8,128)(2,1)S(1)}, u32[]{:S(2)}, u32[]{:S(2)}) collective-permute-start(f16[512,256]{1,0:T(8,128)(2,1)S(1)} %pad_maximum_fusion.3), channel_id=1, source_target_pairs={{0,1},{1,0},{2,3},{3,2},{4,5},{5,4},{6,7},{7,6},{8,9},{9,8},{10,11... | collective-permute-start | bytes 786440 | tf_op jit(solution)/shard_map/ppermute | solution.py:17
  17.6 18.7 %collective-permute-start.24 = (f16[256,256]{1,0:T(8,128)(2,1)S(1)}, f16[256,256]{1,0:T(8,128)(2,1)S(1)}, u32[]{:S(2)}, u32[]{:S(2)}) collective-permute-start(f16[256,256]{1,0:T(8,128)(2,1)S(1)} %reduce-precision_convert_fusion), channel_id=1, source_target_pairs={{0,2},{1,3},{2,0},{3,1},{4,6},{5,7},{6,4},{7,5},{8,10},{9,11},{10,... | collective-permute-start | bytes 393224 | tf_op jit(solution)/shard_map/ppermute | solution.py:17
  23.9 12.4 %collective-permute-start.22 = (f16[256,256]{1,0:T(8,128)(2,1)S(1)}, f16[256,256]{1,0:T(8,128)(2,1)S(1)}, u32[]{:S(2)}, u32[]{:S(2)}) collective-permute-start(f16[256,256]{1,0:T(8,128)(2,1)S(1)} %reduce-precision_convert_fusion.3), channel_id=1, source_target_pairs={{0,2},{1,3},{2,0},{3,1},{4,6},{5,7},{6,4},{7,5},{8,10},{9,11},{10,... | collective-permute-start | bytes 393224 | tf_op jit(solution)/shard_map/ppermute | solution.py:17
  29.6 53.9 %collective-permute-start.25 = (f16[528,256]{1,0:T(8,128)(2,1)S(1)}, f16[528,256]{1,0:T(8,128)(2,1)S(1)}, u32[]{:S(2)}, u32[]{:S(2)}) collective-permute-start(f16[528,256]{1,0:T(8,128)(2,1)S(1)} %pad_maximum_fusion.1), channel_id=1, source_target_pairs={{0,2},{1,3},{2,0},{3,1},{4,6},{5,7},{6,4},{7,5},{8,10},{9,11},{10,... | collective-permute-start | bytes 811016 | tf_op jit(solution)/shard_map/ppermute | solution.py:17
  36.5 50.6 %collective-permute-start.28 = (bf16[512,256]{1,0:T(8,128)(2,1)S(1)}, bf16[512,256]{1,0:T(8,128)(2,1)S(1)}, u32[]{:S(2)}, u32[]{:S(2)}) collective-permute-start(bf16[512,256]{1,0:T(8,128)(2,1)S(1)} %pad_maximum_fusion.5.own_ref), channel_id=1, source_target_pairs={{0,508},{4,504},{8,500},{12,496},{16,492},{20,488},{24,484},{28,48... | collective-permute-start | bytes 786440 | tf_op jit(solution)/shard_map/ppermute | solution.py:17
  58.1 23.4 %collective-permute-start.1 = (bf16[512,256]{1,0:T(8,128)(2,1)S(1)}, bf16[512,256]{1,0:T(8,128)(2,1)}, u32[]{:S(2)}, u32[]{:S(2)}) collective-permute-start(bf16[512,256]{1,0:T(8,128)(2,1)S(1)} %param.2), channel_id=1, source_target_pairs={{0,8},{4,12},{8,0},{12,4},{16,24},{20,28},{24,16},{28,20},{32,40},... | collective-permute-start | bytes 786440 | tf_op jit(solution)/shard_map/cond/branch_2_fun/ppermute | solution.py:17
  81.6 19.8 %collective-permute-start.26 = (bf16[528,256]{1,0:T(8,128)(2,1)S(1)}, bf16[528,256]{1,0:T(8,128)(2,1)S(1)}, u32[]{:S(2)}, u32[]{:S(2)}) collective-permute-start(bf16[528,256]{1,0:T(8,128)(2,1)S(1)} %pad_maximum_fusion.mine_ref), channel_id=1, source_target_pairs={{0,1},{1,0},{2,3},{3,2},{4,5},{5,4},{6,7},{7,6},{8,9},{9,8},{10,11... | collective-permute-start | bytes 811016 | tf_op jit(solution)/shard_map/ppermute | solution.py:17
  83.7 17.7 %collective-permute-start.27 = (bf16[528,256]{1,0:T(8,128)(2,1)S(1)}, bf16[528,256]{1,0:T(8,128)(2,1)S(1)}, u32[]{:S(2)}, u32[]{:S(2)}) collective-permute-start(bf16[528,256]{1,0:T(8,128)(2,1)S(1)} %pad_maximum_fusion.2.second_ref), channel_id=1, source_target_pairs={{0,1},{1,0},{2,3},{3,2},{4,5},{5,4},{6,7},{7,6},{8,9},{9,8},{10,11... | collective-permute-start | bytes 811016 | tf_op jit(solution)/shard_map/ppermute | solution.py:17
  88.1 13.3 %copy-start.1 = (f32[8]{0:T(128)S(1)}, f32[8]{0:T(128)}, u32[]{:S(2)}) copy-start(f32[8]{0:T(128)} %widths_ref.1) | copy-start | bytes 100
  88.1 13.3 %copy-start.2 = (s32[128]{0:T(128)S(1)}, s32[128]{0:T(128)}, u32[]{:S(2)}) copy-start(s32[128]{0:T(128)} %fill_ref.1) | copy-start | bytes 1540
  88.1 13.2 %collective-permute-start.15 = (bf16[512,256]{1,0:T(8,128)(2,1)S(1)}, bf16[512,256]{1,0:T(8,128)(2,1)S(1)}, u32[]{:S(2)}, u32[]{:S(2)}) collective-permute-start(bf16[512,256]{1,0:T(8,128)(2,1)S(1)} %param.18), channel_id=1, source_target_pairs={{0,320},{4,324},{8,328},{12,332},{16,336},{20,340},{24,344},{28,34... | collective-permute-start | bytes 786440 | tf_op jit(solution)/shard_map/cond/branch_10_fun/ppermute | solution.py:17
  107.0 7.7 %all-to-all-start = ((f32[4,2,512]{2,1,0:T(2,128)}), f32[4,2,512]{2,1,0:T(2,128)S(1)}, u32[]{:S(2)}, u32[]{:S(2)}) async-start(f32[4,2,512]{2,1,0:T(2,128)} %shard_map.77), calls=%async_computation | async-start | bytes 32768 | tf_op jit(solution)/shard_map/all_to_all | solution.py:159

commit v4 on v3

--- a/solution.py
+++ b/solution.py
@@ -109,22 +109,12 @@
     cell_pos = lax.axis_index("cell")
     comps = loadings.shape[1]
     far = blocks - 1
-    other = jnp.where(plan[0] == far, plan[1], plan[0])
-    where = jnp.stack([gene_pos, cell_pos, jnp.bitwise_xor(cell_pos, far), jnp.bitwise_xor(cell_pos, other)])
     first = gene_pos * share
-    forward = jnp.bitwise_and(other, 4) != 0
-    path = jnp.where(forward, jnp.bitwise_xor(other, far), other)
-    early = jnp.where(forward, 0, path % 4)
-    late = jnp.where(forward, path % 4, 0)
-    across_plane = path // 8
     index = jnp.pad(width_index.reshape(-1, comps), ((0, EXTRA - share // comps), (0, 0)))
 
-    chunks = 2
-    half = share // chunks
-
-    def partial(shard, chunk):
-        begin = jnp.bitwise_xor(gene_pos, shard) * share + chunk * half
-        rows = lax.dynamic_slice_in_dim(counts, begin, half, 0)
+    def partial(shard):
+        begin = jnp.bitwise_xor(gene_pos, shard) * share
+        rows = lax.dynamic_slice_in_dim(counts, begin, share, 0)
         return jnp.dot(rows, loadings, preferred_element_type=jnp.float32)
 
     def narrow(x):
@@ -133,24 +123,28 @@
     def widen(x):
         return x.astype(jnp.float32)
 
-    near = [swapped(jnp.concatenate([narrow(partial(1, c)), narrow(partial(3, c))]), "gene", 1) for c in range(chunks)]
-    pair = [
-        (narrow(partial(0, c) + widen(near[c][:half])), narrow(partial(2, c) + widen(near[c][half:])))
-        for c in range(chunks)
-    ]
-    wide = [swapped(pair[c][1], "gene", 2) for c in range(chunks)]
-    back = swapped(jnp.concatenate([pair[c][0] for c in range(chunks)] + [index.astype(jnp.float16)]), "gene", 2)
-    wide[0], forward, early, late, across_plane, where = lax.optimization_barrier((wide[0], forward, early, late, across_plane, where))
-    scores = jnp.concatenate([widen(pair[c][0]) + widen(wide[c]) for c in range(chunks)]).astype(jnp.bfloat16)
+    near = swapped(narrow(partial(3)), "gene", 1)
+    nearest = swapped(narrow(partial(1)), "gene", 1)
+    theirs = narrow(partial(2) + widen(near))
+    ours = partial(0) + widen(nearest)
+    wide = swapped(theirs, "gene", 2)
+    plan, ours = lax.optimization_barrier((plan, ours))
+    other = jnp.where(plan[0] == far, plan[1], plan[0])
+    where = jnp.stack([gene_pos, cell_pos, jnp.bitwise_xor(cell_pos, far), jnp.bitwise_xor(cell_pos, other)])
+    forward = jnp.bitwise_and(other, 4) != 0
+    path = jnp.where(forward, jnp.bitwise_xor(other, far), other)
+    early = jnp.where(forward, 0, path % 4)
+    late = jnp.where(forward, path % 4, 0)
+    across_plane = path // 8
+    wide, ours, forward, early, late, across_plane, where = lax.optimization_barrier((wide, ours, forward, early, late, across_plane, where))
+    scores = (ours + widen(wide)).astype(jnp.bfloat16)
+    mine = jnp.concatenate([scores, index.astype(jnp.bfloat16)])
     partner = swapped(scores, "cell", far)
     moved = chosen(scores, "cell", early, 1, 4)
-    back, moved = lax.optimization_barrier((back, moved))
-    second = jnp.concatenate([widen(pair[c][1]) + widen(back[c * half : (c + 1) * half]) for c in range(chunks)]).astype(jnp.bfloat16)
-    mine = [
-        jnp.concatenate([scores, index.astype(jnp.bfloat16)]),
-        jnp.concatenate([second, back[share:].astype(jnp.bfloat16)]),
-    ]
-    beside = [swapped(part, "gene", 1) for part in mine]
+    mine, moved = lax.optimization_barrier((mine, moved))
+    across, second, beside = [swapped(mine, "gene", step) for step in (3, 2, 1)]
+    mine = [mine, second]
+    beside = [beside, across]
     moved = jnp.where(forward, partner, moved)
     moved = chosen(moved, "cell", late, 1, 4)
     moved = chosen(moved, "cell", across_plane, 8, blocks // 8)

time: 117 us -> 119 us (1.017)
  waiting for transfers between devices: 34.4 us -> 39.1 us
  matrix products: 11 us -> 6.8 us
  starting transfers between devices: 56.9 us -> 58.6 us
    ppermute x10 -> x9, waiting for transfers between devices: 30.6 us -> 35.3 us  [swapped(): return lax.ppermute(value, axis, pairs)]
    dot_general x8 -> x4, matrix products: 11 us -> 6.8 us  [partial(): return jnp.dot(rows, loadings, preferred_element_type=jnp.float32)]
    ppermute x10 -> x9, starting transfers between devices: 53.6 us -> 54.8 us  [swapped(): return lax.ppermute(value, axis, pairs)]
  transfers between devices with their start and end apart: 11 -> 10, of which waited for: 4 -> 6; matrix products, arithmetic and copies ran while one was open for 9% -> 6% of each run, Pallas kernels for 0% -> 0%
where the time goes in v4:
time: 119 us; the launch traced here: 118 us
  starting transfers between devices  58.6 us (49%)
  waiting for transfers between devices  39.1 us (33%)
  matrix products  6.8 us (6%)
  Pallas kernels  5.64 us (5%)
  between operations  2.93 us (2%)
  other arithmetic  2.45 us (2%)
  local copies, waits for them, and re-layouts  2.32 us (2%)
    ppermute x9, starting transfers between devices, swapped(): return lax.ppermute(value, axis, pairs)  54.8 us
    ppermute x9, waiting for transfers between devices, swapped(): return lax.ppermute(value, axis, pairs)  35.3 us
    dot_general x4, matrix products, partial(): return jnp.dot(rows, loadings, preferred_element_type=jnp.float32)  6.8 us
    pallas_call x1, Pallas kernels, block_terms(): pl.pallas_call(functools.partial(terms_kernel, share, comps), out_shape=j...  5.64 us
    all_to_all x1, starting transfers between devices, per_device(): both = lax.all_to_all(terms, 'gene', 0, 0)  3.84 us
    all_to_all x1, waiting for transfers between devices, per_device(): both = lax.all_to_all(terms, 'gene', 0, 0)  3.82 us
  transfers between devices with their start and end apart: 10, of which 6 were waited for; matrix products, arithmetic and copies ran while one was open for 6% of the time, Pallas kernels for 0%

profile of v4, /device:TPU:1, one launch (start us, length us, event | category | flops | bytes accessed | tf_op | source)
XLA Modules:
  0.0 118.0 jit_solution(11588371800982221262)
XLA Ops:
  0.6 0.0 copy-start
  0.7 1.0 copy-done
  1.7 0.0 copy-start.4
  1.7 1.7 %fusion = f16[512,256]{1,0:T(8,128)(2,1)S(1)} fusion(bf16[1024,256]{1,0:T(8,128)(2,1)S(1)} %copy-done, bf16[2048,1024]{1,0:T(8,128)(2,1)} %param.30, s32[]{:T(128)S(6)} %select_n.63), kind=kOutput, calls=%fused_computation.2 | convolution fusion | flops 268697600 | bytes 1835012 | tf_op jit(solution)/shard_map/dot_general | solution.py:118
  3.4 0.0 copy-start.3
  3.4 4.4 %collective-permute-start.21 = (f16[512,256]{1,0:T(8,128)(2,1)S(1)}, f16[512,256]{1,0:T(8,128)(2,1)S(1)}, u32[]{:S(2)}, u32[]{:S(2)}) collective-permute-start(f16[512,256]{1,0:T(8,128)(2,1)S(1)} %fusion), channel_id=1, source_target_pairs={{0,1},{1,0},{2,3},{3,2},{4,5},{5,4},{6,7},{7,6},{8,9},{9,8},{10,11... | collective-permute-start | bytes 786440 | tf_op jit(solution)/shard_map/ppermute | solution.py:17
  7.8 1.7 %fusion.1 = f16[512,256]{1,0:T(8,128)(2,1)S(1)} fusion(bf16[1024,256]{1,0:T(8,128)(2,1)S(1)} %copy-done, bf16[2048,1024]{1,0:T(8,128)(2,1)} %param.30, s32[]{:T(128)S(6)} %select_n.65), kind=kOutput, calls=%fused_computation.3 | convolution fusion | flops 268697600 | bytes 1835012 | tf_op jit(solution)/shard_map/dot_general | solution.py:118
  9.5 1.9 %collective-permute-start.23 = (f16[512,256]{1,0:T(8,128)(2,1)S(1)}, f16[512,256]{1,0:T(8,128)(2,1)S(1)}, u32[]{:S(2)}, u32[]{:S(2)}) collective-permute-start(f16[512,256]{1,0:T(8,128)(2,1)S(1)} %fusion.1), channel_id=1, source_target_pairs={{0,1},{1,0},{2,3},{3,2},{4,5},{5,4},{6,7},{7,6},{8,9},{9,8},{10,11... | collective-permute-start | bytes 786440 | tf_op jit(solution)/shard_map/ppermute | solution.py:17
  11.4 0.1 collective-permute-done.21
  11.5 1.7 %reduce-precision_convert_fusion = f16[512,256]{1,0:T(8,128)(2,1)S(1)} fusion(f16[512,256]{1,0:T(8,128)(2,1)S(1)} %collective-permute-done.21, bf16[1024,256]{1,0:T(8,128)(2,1)S(1)} %copy-done, bf16[2048,1024]{1,0:T(8,128)(2,1)} %param.30, s32[]{:T(128)S(6)} %select_n.62), kind=kOutput, calls=%fused_computation.14 | convolution fusion | flops 268959744 | bytes 2097156 | tf_op jit(solution)/shard_map/dot_general | solution.py:118
  13.3 7.1 %collective-permute-start.22 = (f16[512,256]{1,0:T(8,128)(2,1)S(1)}, f16[512,256]{1,0:T(8,128)(2,1)S(1)}, u32[]{:S(2)}, u32[]{:S(2)}) collective-permute-start(f16[512,256]{1,0:T(8,128)(2,1)S(1)} %reduce-precision_convert_fusion), channel_id=1, source_target_pairs={{0,2},{1,3},{2,0},{3,1},{4,6},{5,7},{6,4},{7,5},{8,10},{9,11},{10,... | collective-permute-start | bytes 786440 | tf_op jit(solution)/shard_map/ppermute | solution.py:17
  20.3 0.0 collective-permute-done.23
  20.3 1.7 %convert_add_fusion = f32[512,256]{1,0:T(8,128)S(1)} fusion(f16[512,256]{1,0:T(8,128)(2,1)S(1)} %collective-permute-done.23, bf16[1024,256]{1,0:T(8,128)(2,1)S(1)} %copy-done, bf16[2048,1024]{1,0:T(8,128)(2,1)} %param.30, s32[]{:T(128)S(6)} %select_n.64), kind=kOutput, calls=%fused_computation.13 | convolution fusion | flops 268697600 | bytes 2359300 | tf_op jit(solution)/shard_map/dot_general | solution.py:118
  22.0 0.0 copy-done.4
  22.0 0.6 fusion.18
  24.7 0.1 pad_add_fusion.where_ref
  24.8 2.2 %collective-permute-done.22 = f16[512,256]{1,0:T(8,128)(2,1)S(1)} collective-permute-done((f16[512,256]{1,0:T(8,128)(2,1)S(1)}, f16[512,256]{1,0:T(8,128)(2,1)S(1)}, u32[]{:S(2)}, u32[]{:S(2)}) %collective-permute-start.22) | collective-permute-done | bytes 262176 | tf_op jit(solution)/shard_map/ppermute | solution.py:17
  26.9 0.1 add_convert_fusion.own_ref
  27.0 22.2 %collective-permute-start.27 = (bf16[512,256]{1,0:T(8,128)(2,1)S(1)}, bf16[512,256]{1,0:T(8,128)(2,1)S(1)}, u32[]{:S(2)}, u32[]{:S(2)}) collective-permute-start(bf16[512,256]{1,0:T(8,128)(2,1)S(1)} %add_convert_fusion.own_ref), channel_id=1, source_target_pairs={{0,508},{4,504},{8,500},{12,496},{16,492},{20,488},{24,484},{28,48... | collective-permute-start | bytes 786440 | tf_op jit(solution)/shard_map/ppermute | solution.py:17
  49.2 0.0 copy-done.3
  49.3 23.9 %conditional.3 = (bf16[512,256]{1,0:T(8,128)(2,1)}) conditional(s32[]{:T(128)} %clamp.9, bf16[512,256]{1,0:T(8,128)(2,1)S(1)} %add_convert_fusion.own_ref, bf16[512,256]{1,0:T(8,128)(2,1)S(1)} %add_convert_fusion.own_ref, bf16[512,256]{1,0:T(8,128)(2,1)S(1)} %add_convert_fusion.own_ref, ...), branch_computations={%region_0.1_spmd, %region_1.2_spmd, %region_2.3_spmd, %region_3.4_... | conditional | bytes 1048624 | solution.py:24
  49.3 5.2 %collective-permute-start.1 = (bf16[512,256]{1,0:T(8,128)(2,1)S(1)}, bf16[512,256]{1,0:T(8,128)(2,1)}, u32[]{:S(2)}, u32[]{:S(2)}) collective-permute-start(bf16[512,256]{1,0:T(8,128)(2,1)S(1)} %param.2), channel_id=1, source_target_pairs={{0,8},{4,12},{8,0},{12,4},{16,24},{20,28},{24,16},{28,20},{32,40},... | collective-permute-start | bytes 786440 | tf_op jit(solution)/shard_map/cond/branch_2_fun/ppermute | solution.py:17
  54.5 18.7 %collective-permute-done.1 = bf16[512,256]{1,0:T(8,128)(2,1)} collective-permute-done((bf16[512,256]{1,0:T(8,128)(2,1)S(1)}, bf16[512,256]{1,0:T(8,128)(2,1)}, u32[]{:S(2)}, u32[]{:S(2)}) %collective-permute-start.1) | collective-permute-done | bytes 262176 | tf_op jit(solution)/shard_map/cond/branch_2_fun/ppermute | solution.py:17
  73.2 4.5 %collective-permute-start.26 = (bf16[528,256]{1,0:T(8,128)(2,1)S(1)}, bf16[528,256]{1,0:T(8,128)(2,1)S(1)}, u32[]{:S(2)}, u32[]{:S(2)}) collective-permute-start(bf16[528,256]{1,0:T(8,128)(2,1)S(1)} %fusion.9.mine_ref), channel_id=1, source_target_pairs={{0,3},{1,2},{2,1},{3,0},{4,7},{5,6},{6,5},{7,4},{8,11},{9,10},{10,... | collective-permute-start | bytes 811016 | tf_op jit(solution)/shard_map/ppermute | solution.py:17
  77.7 5.7 %collective-permute-start.25 = (bf16[528,256]{1,0:T(8,128)(2,1)S(1)}, bf16[528,256]{1,0:T(8,128)(2,1)S(1)}, u32[]{:S(2)}, u32[]{:S(2)}) collective-permute-start(bf16[528,256]{1,0:T(8,128)(2,1)S(1)} %fusion.9.mine_ref), channel_id=1, source_target_pairs={{0,1},{1,0},{2,3},{3,2},{4,5},{5,4},{6,7},{7,6},{8,9},{9,8},{10,11... | collective-permute-start | bytes 811016 | tf_op jit(solution)/shard_map/ppermute | solution.py:17
  83.5 1.9 %collective-permute-start.24 = (bf16[528,256]{1,0:T(8,128)(2,1)S(1)}, bf16[528,256]{1,0:T(8,128)(2,1)S(1)}, u32[]{:S(2)}, u32[]{:S(2)}) collective-permute-start(bf16[528,256]{1,0:T(8,128)(2,1)S(1)} %fusion.9.mine_ref), channel_id=1, source_target_pairs={{0,2},{1,3},{2,0},{3,1},{4,6},{5,7},{6,4},{7,5},{8,10},{9,11},{10,... | collective-permute-start | bytes 811016 | tf_op jit(solution)/shard_map/ppermute | solution.py:17
  85.4 0.0 collective-permute-done.27.far_ref
  85.4 1.0 broadcast_select_fusion
  86.4 0.0 copy-start.1
  86.4 0.0 copy-start.2
  86.5 10.9 %conditional.5 = (bf16[512,256]{1,0:T(8,128)(2,1)S(1)}) conditional(s32[]{:T(128)} %clamp.10, bf16[512,256]{1,0:T(8,128)(2,1)S(1)} %get-tuple-element.82, bf16[512,256]{1,0:T(8,128)(2,1)S(1)} %get-tuple-element.82, bf16[512,256]{1,0:T(8,128)(2,1)S(1)} %get-tuple-element.82, ...), branch_computations={%region_8.9_spmd, %region_9.10_spmd, %region_10.11_spmd, %region_1... | conditional | bytes 1572912 | solution.py:24
  86.5 1.9 %collective-permute-start.18 = (bf16[512,256]{1,0:T(8,128)(2,1)S(1)}, bf16[512,256]{1,0:T(8,128)(2,1)S(1)}, u32[]{:S(2)}, u32[]{:S(2)}) collective-permute-start(bf16[512,256]{1,0:T(8,128)(2,1)S(1)} %param.21), channel_id=1, source_target_pairs={{0,416},{4,420},{8,424},{12,428},{16,432},{20,436},{24,440},{28,44... | collective-permute-start | bytes 786440 | tf_op jit(solution)/shard_map/cond/branch_13_fun/ppermute | solution.py:17
  88.4 8.9 %collective-permute-done.18 = bf16[512,256]{1,0:T(8,128)(2,1)S(1)} collective-permute-done((bf16[512,256]{1,0:T(8,128)(2,1)S(1)}, bf16[512,256]{1,0:T(8,128)(2,1)S(1)}, u32[]{:S(2)}, u32[]{:S(2)}) %collective-permute-start.18) | collective-permute-done | bytes 262176 | tf_op jit(solution)/shard_map/cond/branch_13_fun/ppermute | solution.py:17
  97.4 0.0 collective-permute-done.26.across_ref
  97.4 0.0 collective-permute-done.25.beside_ref
  97.4 5.3 %collective-permute-done.24.second_ref = bf16[528,256]{1,0:T(8,128)(2,1)S(1)} collective-permute-done((bf16[528,256]{1,0:T(8,128)(2,1)S(1)}, bf16[528,256]{1,0:T(8,128)(2,1)S(1)}, u32[]{:S(2)}, u32[]{:S(2)}) %collective-permute-start.24) | collective-permute-done | bytes 270368 | tf_op jit(solution)/shard_map/ppermute | solution.py:17
  102.8 0.0 copy-done.1
  102.8 0.0 copy-done.2
  102.8 5.6 %shard_map.77 = f32[4,2,512]{2,1,0:T(2,128)} custom-call(s32[4]{0:T(128)S(1)} %pad_add_fusion.where_ref, s32[128]{0:T(128)S(1)} %copy-done.2, f32[8]{0:T(128)S(1)} %copy-done.1, bf16[528,256]{1,0:T(8,128)(2,1)S(1)} %fusion.9.mine_ref, bf16[528,256]{1,0:T(8,128)(2,1)S(1)} %collective-permute-done.24.second_ref, ...), custom_call_target="tpu_custom_call" | custom-call | tf_op jit(solution)/shard_map/pallas_call | solution.py:89
  108.4 3.8 %all-to-all-start = ((f32[4,2,512]{2,1,0:T(2,128)}), f32[4,2,512]{2,1,0:T(2,128)S(1)}, u32[]{:S(2)}, u32[]{:S(2)}) async-start(f32[4,2,512]{2,1,0:T(2,128)} %shard_map.77), calls=%async_computation | async-start | bytes 32768 | tf_op jit(solution)/shard_map/all_to_all | solution.py:153
  112.2 0.6 dynamic_slice.15
  112.9 3.8 %all-to-all-done = f32[4,2,512]{2,1,0:T(2,128)S(1)} async-done(((f32[4,2,512]{2,1,0:T(2,128)}), f32[4,2,512]{2,1,0:T(2,128)S(1)}, u32[]{:S(2)}, u32[]{:S(2)}) %all-to-all-start) | async-done | bytes 16416 | tf_op jit(solution)/shard_map/all_to_all | solution.py:153
  116.7 1.3 %sqrt_select_fusion = (f32[512]{0:T(512)}, f32[512]{0:T(512)}) fusion(f32[512]{0:T(512)S(1)} %get-tuple-element.75, s32[]{:T(128)} %bitcast, s32[]{:T(128)S(6)} %mul.13, f32[512]{0:T(512)S(1)} %get-tuple-element.76), kind=kLoop, calls=%fused_computation.19 | loop fusion | flops 2560 | bytes 8200 | tf_op jit(solution)/shard_map/jit(_where)/select_n | solution.py:158
  (6 shorter events, 0.1 us)
Async XLA Ops:
  0.6 1.0 copy-start
  1.7 20.3 %copy-start.4 = (s32[2]{0:T(128)S(1)}, s32[2]{0:T(128)}, u32[]{:S(2)}) copy-start(s32[2]{0:T(128)} %param.35) | copy-start | bytes 28
  3.4 45.8 %copy-start.3 = (s32[512]{0:T(512)S(1)}, s32[512]{0:T(512)}, u32[]{:S(2)}) copy-start(s32[512]{0:T(512)} %param.33) | copy-start | bytes 6148
  3.4 8.1 %collective-permute-start.21 = (f16[512,256]{1,0:T(8,128)(2,1)S(1)}, f16[512,256]{1,0:T(8,128)(2,1)S(1)}, u32[]{:S(2)}, u32[]{:S(2)}) collective-permute-start(f16[512,256]{1,0:T(8,128)(2,1)S(1)} %fusion), channel_id=1, source_target_pairs={{0,1},{1,0},{2,3},{3,2},{4,5},{5,4},{6,7},{7,6},{8,9},{9,8},{10,11... | collective-permute-start | bytes 786440 | tf_op jit(solution)/shard_map/ppermute | solution.py:17
  9.5 10.8 %collective-permute-start.23 = (f16[512,256]{1,0:T(8,128)(2,1)S(1)}, f16[512,256]{1,0:T(8,128)(2,1)S(1)}, u32[]{:S(2)}, u32[]{:S(2)}) collective-permute-start(f16[512,256]{1,0:T(8,128)(2,1)S(1)} %fusion.1), channel_id=1, source_target_pairs={{0,1},{1,0},{2,3},{3,2},{4,5},{5,4},{6,7},{7,6},{8,9},{9,8},{10,11... | collective-permute-start | bytes 786440 | tf_op jit(solution)/shard_map/ppermute | solution.py:17
  13.3 13.7 %collective-permute-start.22 = (f16[512,256]{1,0:T(8,128)(2,1)S(1)}, f16[512,256]{1,0:T(8,128)(2,1)S(1)}, u32[]{:S(2)}, u32[]{:S(2)}) collective-permute-start(f16[512,256]{1,0:T(8,128)(2,1)S(1)} %reduce-precision_convert_fusion), channel_id=1, source_target_pairs={{0,2},{1,3},{2,0},{3,1},{4,6},{5,7},{6,4},{7,5},{8,10},{9,11},{10,... | collective-permute-start | bytes 786440 | tf_op jit(solution)/shard_map/ppermute | solution.py:17
  27.0 58.4 %collective-permute-start.27 = (bf16[512,256]{1,0:T(8,128)(2,1)S(1)}, bf16[512,256]{1,0:T(8,128)(2,1)S(1)}, u32[]{:S(2)}, u32[]{:S(2)}) collective-permute-start(bf16[512,256]{1,0:T(8,128)(2,1)S(1)} %add_convert_fusion.own_ref), channel_id=1, source_target_pairs={{0,508},{4,504},{8,500},{12,496},{16,492},{20,488},{24,484},{28,48... | collective-permute-start | bytes 786440 | tf_op jit(solution)/shard_map/ppermute | solution.py:17
  49.3 23.9 %collective-permute-start.1 = (bf16[512,256]{1,0:T(8,128)(2,1)S(1)}, bf16[512,256]{1,0:T(8,128)(2,1)}, u32[]{:S(2)}, u32[]{:S(2)}) collective-permute-start(bf16[512,256]{1,0:T(8,128)(2,1)S(1)} %param.2), channel_id=1, source_target_pairs={{0,8},{4,12},{8,0},{12,4},{16,24},{20,28},{24,16},{28,20},{32,40},... | collective-permute-start | bytes 786440 | tf_op jit(solution)/shard_map/cond/branch_2_fun/ppermute | solution.py:17
  73.2 24.2 %collective-permute-start.26 = (bf16[528,256]{1,0:T(8,128)(2,1)S(1)}, bf16[528,256]{1,0:T(8,128)(2,1)S(1)}, u32[]{:S(2)}, u32[]{:S(2)}) collective-permute-start(bf16[528,256]{1,0:T(8,128)(2,1)S(1)} %fusion.9.mine_ref), channel_id=1, source_target_pairs={{0,3},{1,2},{2,1},{3,0},{4,7},{5,6},{6,5},{7,4},{8,11},{9,10},{10,... | collective-permute-start | bytes 811016 | tf_op jit(solution)/shard_map/ppermute | solution.py:17
  77.7 19.7 %collective-permute-start.25 = (bf16[528,256]{1,0:T(8,128)(2,1)S(1)}, bf16[528,256]{1,0:T(8,128)(2,1)S(1)}, u32[]{:S(2)}, u32[]{:S(2)}) collective-permute-start(bf16[528,256]{1,0:T(8,128)(2,1)S(1)} %fusion.9.mine_ref), channel_id=1, source_target_pairs={{0,1},{1,0},{2,3},{3,2},{4,5},{5,4},{6,7},{7,6},{8,9},{9,8},{10,11... | collective-permute-start | bytes 811016 | tf_op jit(solution)/shard_map/ppermute | solution.py:17
  83.5 19.3 %collective-permute-start.24 = (bf16[528,256]{1,0:T(8,128)(2,1)S(1)}, bf16[528,256]{1,0:T(8,128)(2,1)S(1)}, u32[]{:S(2)}, u32[]{:S(2)}) collective-permute-start(bf16[528,256]{1,0:T(8,128)(2,1)S(1)} %fusion.9.mine_ref), channel_id=1, source_target_pairs={{0,2},{1,3},{2,0},{3,1},{4,6},{5,7},{6,4},{7,5},{8,10},{9,11},{10,... | collective-permute-start | bytes 811016 | tf_op jit(solution)/shard_map/ppermute | solution.py:17
  86.4 16.3 %copy-start.1 = (f32[8]{0:T(128)S(1)}, f32[8]{0:T(128)}, u32[]{:S(2)}) copy-start(f32[8]{0:T(128)} %widths_ref.1) | copy-start | bytes 100
  86.4 16.3 %copy-start.2 = (s32[128]{0:T(128)S(1)}, s32[128]{0:T(128)}, u32[]{:S(2)}) copy-start(s32[128]{0:T(128)} %fill_ref.1) | copy-start | bytes 1540
  86.5 10.9 %collective-permute-start.18 = (bf16[512,256]{1,0:T(8,128)(2,1)S(1)}, bf16[512,256]{1,0:T(8,128)(2,1)S(1)}, u32[]{:S(2)}, u32[]{:S(2)}) collective-permute-start(bf16[512,256]{1,0:T(8,128)(2,1)S(1)} %param.21), channel_id=1, source_target_pairs={{0,416},{4,420},{8,424},{12,428},{16,432},{20,436},{24,440},{28,44... | collective-permute-start | bytes 786440 | tf_op jit(solution)/shard_map/cond/branch_13_fun/ppermute | solution.py:17
  108.4 8.3 %all-to-all-start = ((f32[4,2,512]{2,1,0:T(2,128)}), f32[4,2,512]{2,1,0:T(2,128)S(1)}, u32[]{:S(2)}, u32[]{:S(2)}) async-start(f32[4,2,512]{2,1,0:T(2,128)} %shard_map.77), calls=%async_computation | async-start | bytes 32768 | tf_op jit(solution)/shard_map/all_to_all | solution.py:153
